TPU v7x, 256 devices: a whole 4x4x8 slice. The times are simulated.
256 devices in a mesh: dp: 16 (over z, core), graph: 16 (over y, x).
Axes of the slice: x: 4, y: 4, z: 8, core: 2. Of those that a mesh axis runs over, the one named last changes fastest.
Arguments:
- node_feats: bfloat16 [16, 256, 3200], P('dp', 'graph'), may hold values from -6 to 6
- source: int32 [16, 2048], P('dp', 'graph'), may hold values from 0 to 255
- target: int32 [16, 2048], P('dp', 'graph'), may hold values from 0 to 255
- rotation: bfloat16 [16, 165, 2048], P('dp', None, 'graph'), may hold values from -6 to 6
- radial: bfloat16 [16, 2048, 640], P('dp', 'graph'), may hold values from 0.25 to 1.75
- edge_count: int32 [16, 16], P('dp', 'graph'), may hold values from 16 to 128, as said below
- cotangent: bfloat16 [16, 256, 3200], P('dp', 'graph'), may hold values from -6 to 6
- weight_zero: bfloat16 [640, 640], replicated, may hold values from -0.25 to 0.25
- weight_first: bfloat16 [2, 512, 512], replicated, may hold values from -0.1875 to 0.1875
- weight_second: bfloat16 [2, 384, 384], replicated, may hold values from -0.21875 to 0.21875
Outputs:
- node_out: bfloat16 [16, 256, 3200], P('dp', 'graph')
- node_grad: bfloat16 [16, 256, 3200], P('dp', 'graph')
- grad_zero: float32 [640, 640], replicated
- grad_first: float32 [2, 512, 512], replicated
- grad_second: float32 [2, 384, 384], replicated
Inputs may be any that keep to these rules, and one draw needn't show every extreme that they name: In each device's 128 slots the first edge_count are live; in every batch some index of graph has all 128 live.
All inputs are finite; a program needn't handle non-finite values.
Results may differ from a plain program's by a relative error of at most 0.019.
Values may be sent and summed in bfloat16 or wider, within the bound.
A program may use at most 128 MiB of HBM per device.

v0:
```python
import math

import jax
import jax.numpy as jnp
import numpy as np
from jax import lax
from jax.sharding import PartitionSpec as P

TILE = 128


ZERO_ORDER = [0, 2, 6, 12, 20]
PLUS_FIRST = [3, 7, 13, 21]
MINUS_FIRST = [1, 5, 11, 19]
PLUS_SECOND = [8, 14, 22]
MINUS_SECOND = [4, 10, 18]


def rotate_blocks(values, rot_rows, transposed):
    results = []
    offset = 0
    for degree in range(5):
        order_size = 2 * degree + 1
        block = rot_rows[:, offset : offset + order_size * order_size].reshape(
            -1, order_size, order_size
        )
        if transposed:
            block = jnp.swapaxes(block, 1, 2)
        coef_piece = values[:, degree * degree : (degree + 1) * (degree + 1), :].astype(jnp.float32)
        total = block[:, :, 0, None] * coef_piece[:, None, 0, :]
        for inner in range(1, order_size):
            total = total + block[:, :, inner, None] * coef_piece[:, None, inner, :]
        results.append(total / math.sqrt(order_size))
        offset += order_size * order_size
    return jnp.concatenate(results, axis=1)


def scale_degrees(values, rad_rows):
    pieces = []
    for degree in range(5):
        pieces.append(
            values[:, degree * degree : (degree + 1) * (degree + 1), :]
            * rad_rows[:, degree, None, :]
        )
    return jnp.concatenate(pieces, axis=1)


def pick_rows(values, indices):
    return values[:, np.array(indices), :].reshape(values.shape[0], len(indices) * values.shape[2])


def join_groups(groups, channels):
    edge_rows = groups[0][1].shape[0]
    columns = [jnp.zeros((edge_rows, channels), jnp.float32)] * 25
    for indices, array in groups:
        shaped = array.reshape(edge_rows, len(indices), channels)
        for position, coef_index in enumerate(indices):
            columns[coef_index] = shaped[:, position, :]
    return jnp.stack(columns, axis=1)


def contract_rows(left, right):
    return lax.dot_general(
        left, right, (((0,), (0,)), ((), ())), preferred_element_type=jnp.float32
    )


def times_transposed(left, weight):
    return lax.dot_general(
        left, weight, (((1,), (1,)), ((), ())), preferred_element_type=jnp.float32
    )


def plane_forward(active, weight_zero, weight_first, weight_second):
    channels = active.shape[2]
    zero_part = pick_rows(active, ZERO_ORDER)
    plus_one = pick_rows(active, PLUS_FIRST)
    minus_one = pick_rows(active, MINUS_FIRST)
    plus_two = pick_rows(active, PLUS_SECOND)
    minus_two = pick_rows(active, MINUS_SECOND)
    out_zero = jnp.dot(zero_part, weight_zero, preferred_element_type=jnp.float32)
    out_plus_one = jnp.dot(plus_one, weight_first[0], preferred_element_type=jnp.float32) - jnp.dot(
        minus_one, weight_first[1], preferred_element_type=jnp.float32
    )
    out_minus_one = jnp.dot(
        minus_one, weight_first[0], preferred_element_type=jnp.float32
    ) + jnp.dot(plus_one, weight_first[1], preferred_element_type=jnp.float32)
    out_plus_two = jnp.dot(
        plus_two, weight_second[0], preferred_element_type=jnp.float32
    ) - jnp.dot(minus_two, weight_second[1], preferred_element_type=jnp.float32)
    out_minus_two = jnp.dot(
        minus_two, weight_second[0], preferred_element_type=jnp.float32
    ) + jnp.dot(plus_two, weight_second[1], preferred_element_type=jnp.float32)
    return join_groups(
        [
            (ZERO_ORDER, out_zero),
            (PLUS_FIRST, out_plus_one),
            (MINUS_FIRST, out_minus_one),
            (PLUS_SECOND, out_plus_two),
            (MINUS_SECOND, out_minus_two),
        ],
        channels,
    )


def plane_backward(active, upstream, weight_zero, weight_first, weight_second):
    channels = active.shape[2]
    zero_part = pick_rows(active, ZERO_ORDER)
    plus_one = pick_rows(active, PLUS_FIRST)
    minus_one = pick_rows(active, MINUS_FIRST)
    plus_two = pick_rows(active, PLUS_SECOND)
    minus_two = pick_rows(active, MINUS_SECOND)
    up_zero = pick_rows(upstream, ZERO_ORDER)
    up_plus_one = pick_rows(upstream, PLUS_FIRST)
    up_minus_one = pick_rows(upstream, MINUS_FIRST)
    up_plus_two = pick_rows(upstream, PLUS_SECOND)
    up_minus_two = pick_rows(upstream, MINUS_SECOND)
    grad_zero = contract_rows(zero_part, up_zero)
    grad_first = jnp.stack(
        [
            contract_rows(plus_one, up_plus_one) + contract_rows(minus_one, up_minus_one),
            contract_rows(plus_one, up_minus_one) - contract_rows(minus_one, up_plus_one),
        ]
    )
    grad_second = jnp.stack(
        [
            contract_rows(plus_two, up_plus_two) + contract_rows(minus_two, up_minus_two),
            contract_rows(plus_two, up_minus_two) - contract_rows(minus_two, up_plus_two),
        ]
    )
    back_zero = times_transposed(up_zero, weight_zero)
    back_plus_one = times_transposed(up_plus_one, weight_first[0]) + times_transposed(
        up_minus_one, weight_first[1]
    )
    back_minus_one = times_transposed(up_minus_one, weight_first[0]) - times_transposed(
        up_plus_one, weight_first[1]
    )
    back_plus_two = times_transposed(up_plus_two, weight_second[0]) + times_transposed(
        up_minus_two, weight_second[1]
    )
    back_minus_two = times_transposed(up_minus_two, weight_second[0]) - times_transposed(
        up_plus_two, weight_second[1]
    )
    d_active = join_groups(
        [
            (ZERO_ORDER, back_zero),
            (PLUS_FIRST, back_plus_one),
            (MINUS_FIRST, back_minus_one),
            (PLUS_SECOND, back_plus_two),
            (MINUS_SECOND, back_minus_two),
        ],
        channels,
    )
    return (d_active, (grad_zero, grad_first, grad_second))


def per_device(
    node_feats,
    source,
    target,
    rotation,
    radial,
    edge_count,
    cotangent,
    weight_zero,
    weight_first,
    weight_second,
):
    node_rows, cot_rows = (
        lax.all_gather(node_feats[0], "graph", axis=0, tiled=True),
        lax.all_gather(cotangent[0], "graph", axis=0, tiled=True),
    )
    nodes = node_rows.shape[0]
    row_width = node_rows.shape[1]
    channels = row_width // 25
    edge_dev = source.shape[1]
    live_count = edge_count[0, 0]
    node_ids = jnp.arange(nodes, dtype=jnp.int32)
    tile_total = edge_dev // TILE

    def tile_compute(step):
        start = step * TILE
        src_tile = source[0]
        dst_tile = target[0]
        slot_ids = start + jnp.arange(TILE, dtype=jnp.int32)
        live = slot_ids < live_count
        src_onehot = (src_tile[:, None] == node_ids[None, :]).astype(jnp.bfloat16)
        dst_onehot = ((dst_tile[:, None] == node_ids[None, :]) & live[:, None]).astype(jnp.bfloat16)
        rot_rows = jnp.transpose(rotation[0]).astype(jnp.float32)
        rad_rows = radial[0].reshape(TILE, 5, channels).astype(jnp.float32)
        gathered = (
            jnp.dot(src_onehot, node_rows, preferred_element_type=jnp.float32)
            .astype(jnp.bfloat16)
            .reshape(TILE, 25, channels)
        )
        active = scale_degrees(rotate_blocks(gathered, rot_rows, False), rad_rows).astype(
            jnp.bfloat16
        )
        edge_msg = plane_forward(active, weight_zero, weight_first, weight_second).astype(
            jnp.bfloat16
        )
        message = (
            rotate_blocks(edge_msg, rot_rows, True).astype(jnp.bfloat16).reshape(TILE, row_width)
        )
        picked = (
            jnp.dot(dst_onehot, cot_rows, preferred_element_type=jnp.float32)
            .astype(jnp.bfloat16)
            .reshape(TILE, 25, channels)
        )
        upstream = rotate_blocks(picked, rot_rows, False).astype(jnp.bfloat16)
        d_active, grads = plane_backward(active, upstream, weight_zero, weight_first, weight_second)
        back = scale_degrees(d_active, rad_rows).astype(jnp.bfloat16)
        edge_grad = (
            rotate_blocks(back, rot_rows, True).astype(jnp.bfloat16).reshape(TILE, row_width)
        )
        return (message, edge_grad, grads, src_onehot, dst_onehot)

    zero_grads = (
        jnp.zeros(weight_zero.shape, jnp.float32),
        jnp.zeros(weight_first.shape, jnp.float32),
        jnp.zeros(weight_second.shape, jnp.float32),
    )

    def tile_step(step, carry):
        out_sum, grad_sum, acc_zero, acc_first, acc_second = carry
        message, edge_grad, grads, src_onehot, dst_onehot = tile_compute(step)
        out_sum = out_sum + contract_rows(dst_onehot, message)
        grad_sum = grad_sum + contract_rows(src_onehot, edge_grad)
        return (out_sum, grad_sum, acc_zero + grads[0], acc_first + grads[1], acc_second + grads[2])

    initial = (
        jnp.zeros((nodes, row_width), jnp.float32),
        jnp.zeros((nodes, row_width), jnp.float32),
    ) + zero_grads
    out_sum, grad_sum, acc_zero, acc_first, acc_second = lax.fori_loop(
        0, tile_total, tile_step, initial
    )
    owned_out, owned_grad = (
        lax.psum_scatter(
            out_sum.astype(jnp.bfloat16), "graph", scatter_dimension=0, tiled=True
        ).astype(jnp.float32),
        lax.psum_scatter(
            grad_sum.astype(jnp.bfloat16), "graph", scatter_dimension=0, tiled=True
        ).astype(jnp.float32),
    )
    scale = 1.0 / math.sqrt(lax.axis_size("dp") * edge_dev * lax.axis_size("graph"))
    flat = (
        jnp.concatenate([acc_zero.reshape(-1), acc_first.reshape(-1), acc_second.reshape(-1)])
        * scale
    )
    summed = lax.psum(flat, ("dp", "graph"))
    size_zero = acc_zero.size
    size_first = acc_first.size
    grad_zero = summed[:size_zero].reshape(acc_zero.shape)
    grad_first = summed[size_zero : size_zero + size_first].reshape(acc_first.shape)
    grad_second = summed[size_zero + size_first :].reshape(acc_second.shape)
    return (
        owned_out.astype(jnp.bfloat16)[None],
        owned_grad.astype(jnp.bfloat16)[None],
        grad_zero,
        grad_first,
        grad_second,
    )


def solution(mesh):
    return jax.shard_map(
        per_device,
        mesh=mesh,
        in_specs=(
            P("dp", "graph", None),
            P("dp", "graph"),
            P("dp", "graph"),
            P("dp", None, "graph"),
            P("dp", "graph", None),
            P("dp", "graph"),
            P("dp", "graph", None),
            P(),
            P(),
            P(),
        ),
        out_specs=(P("dp", "graph", None), P("dp", "graph", None), P(), P(), P()),
        check_vma=False,
    )
```

profile of v0, /device:TPU:1, one launch (start us, length us, event | category | flops | bytes accessed | tf_op | source)
XLA Modules:
  0.0 705.4 jit_solution(14068967827334600998)
XLA Ops:
  31.5 30.9 %all-gather.7.cloned.1.call-done = bf16[1,256,3200]{2,1,0:T(8,128)(2,1)} async-done(((bf16[1,16,3200]{2,1,0:T(8,128)(2,1)}), bf16[1,256,3200]{2,1,0:T(8,128)(2,1)}) %all-gather.7.cloned.1.call-update) | async-done | bytes 1638416 | tf_op jit(solution)/shard_map/all_gather | solution.py:171
  62.4 1.9 convolution_convert_fusion.2
  65.9 47.6 %all-gather.5.cloned.1.call-done = bf16[1,256,3200]{2,1,0:T(8,128)(2,1)} async-done(((bf16[1,16,3200]{2,1,0:T(8,128)(2,1)}), bf16[1,256,3200]{2,1,0:T(8,128)(2,1)}) %all-gather.5.cloned.1.call-update) | async-done | bytes 1638416 | tf_op jit(solution)/shard_map/all_gather | solution.py:170
  113.5 1.9 convolution_convert_fusion.3
  124.6 1.6 slice_bitcast_fusion.44
  126.3 1.6 copy.491
  130.8 1.6 slice_bitcast_fusion.95
  132.4 1.6 copy.428
  137.5 1.6 copy.496
  139.9 1.6 copy.503
  141.5 1.6 copy.511
  143.1 1.6 copy.510
  144.6 1.6 copy.509
  146.2 1.6 copy.508
  147.7 1.6 copy.507
  149.3 1.6 copy.506
  150.9 1.6 copy.505
  152.4 1.6 copy.504
  154.0 1.6 copy.502
  155.6 1.6 copy.501
  174.9 2.0 fusion.49
  177.0 3.3 fusion.32
  185.5 2.6 gather_fusion.5
  188.1 1.7 copy.513
  192.0 1.8 fusion.39
  193.9 1.8 convolution_subtract_fusion.4
  195.7 1.7 copy.524
  199.8 1.8 copy.517
  201.6 1.6 fusion.83
  209.6 2.1 fusion.47
  211.7 3.6 fusion.30
  227.3 1.8 copy.525
  229.0 1.6 copy.538
  230.6 1.6 copy.539
  235.0 1.6 copy.543
  238.0 1.6 copy.541
  242.6 1.6 fusion.82
  246.6 1.6 copy.526
  248.2 1.6 copy.530
  249.7 1.6 copy.529
  255.2 1.6 copy.531
  256.8 1.6 copy.537
  258.3 1.6 copy.536
  259.9 1.6 copy.535
  261.5 1.6 copy.534
  292.2 1.7 copy.468
  293.9 1.6 copy.472
  295.5 1.6 copy.471
  297.0 1.6 copy.470
  298.6 1.6 copy.469
  304.3 1.5 fusion.94
  305.9 2.5 reshape.219
  308.3 6.6 maximum_multiply_fusion
  318.3 2.2 fusion.48
  320.7 2.0 fusion.31
  326.0 2.0 fusion.33
  328.9 1.8 convolution_convert_fusion
  330.8 1.9 convolution_convert_fusion.1
  334.6 251.2 %all-reduce.6.cloned.1.call-done = f32[1228800]{0:T(1024)} async-done(((f32[1228800]{0:T(1024)}), f32[1228800]{0:T(1024)}) %all-reduce.6.cloned.1.call-update) | async-done | bytes 4915216 | tf_op jit(solution)/shard_map/psum | solution.py:251
  588.4 1.6 slice-done.1
  592.9 1.5 slice.1197
  594.4 101.4 %all-reduce.8.cloned.1.call-done = (bf16[256,3200]{1,0:T(8,128)(2,1)}, bf16[256,3200]{1,0:T(8,128)(2,1)}) async-done(((bf16[256,3200]{1,0:T(8,128)(2,1)}, bf16[256,3200]{1,0:T(8,128)(2,1)}), (bf16[256,3200]{1,0:T(8,128)(2,1)}, bf16[256,3200]{1,0:T(8,128)(2,1)})) %all-reduce.8.cloned.1.call-update) | async-done | bytes 3276816
  695.8 1.5 dynamic-slice_bitcast_fusion.1
  697.3 1.5 dynamic-slice_bitcast_fusion
  (519 shorter events, 147.2 us)
Async XLA Ops:
  7.2 13.9 %copy-start.4 = (bf16[640,640]{1,0:T(8,128)(2,1)S(1)}, bf16[640,640]{1,0:T(8,128)(2,1)}, u32[]{:S(2)}) copy-start(bf16[640,640]{1,0:T(8,128)(2,1)} %param.47) | copy-start | bytes 2457604
  7.2 55.2 %all-gather.7.cloned.1.call-start = ((), (), s32[]{:S(2)}) async-start(), calls=%async_computation.2 | async-start | bytes 1740800 | tf_op jit(solution)/shard_map/all_gather | solution.py:171
  7.9 105.6 %all-gather.5.cloned.1.call-start = ((), (), s32[]{:S(2)}) async-start(), calls=%async_computation.1 | async-start | bytes 1740800 | tf_op jit(solution)/shard_map/all_gather | solution.py:170
  8.7 577.2 %all-reduce.6.cloned.1.call-start = ((), (), s32[]{:S(2)}) async-start(), calls=%async_computation | async-start | bytes 9830400 | tf_op jit(solution)/shard_map/psum | solution.py:251
  9.5 110.0 %copy-start.124 = (f32[128]{0:T(128)}, f32[128]{0:T(128)S(1)}, u32[]{:S(2)}) copy-start(f32[128]{0:T(128)S(1)} %slice_bitcast_fusion.124) | copy-start | bytes 1540
  16.4 6.0 copy-start.134
  16.4 6.0 copy-start.135
  16.4 6.6 copy-start.132
  16.5 6.5 copy-start.133
  18.1 44.2 %copy-start.8 = (f32[1,128,640]{1,2,0:T(8,128)}, f32[1,128,640]{1,2,0:T(8,128)S(1)}, u32[]{:S(2)}) copy-start(f32[1,128,640]{1,2,0:T(8,128)S(1)} %copy.423) | copy-start | bytes 983044
  18.2 44.2 %copy-start.126 = (s32[1,128]{1,0:T(1,128)S(1)}, s32[1,128]{1,0:T(1,128)}, u32[]{:S(2)}) copy-start(s32[1,128]{1,0:T(1,128)} %param.42) | copy-start | bytes 1540
  25.4 39.7 %copy-start.128 = (pred[128]{0:T(512)(128)(4,1)}, pred[128]{0:T(512)(128)(4,1)S(1)}, u32[]{:S(2)}) copy-start(pred[128]{0:T(512)(128)(4,1)S(1)} %iota_compare_fusion.3) | copy-start | bytes 388
  64.3 49.3 %copy-start.130 = (s32[1,128]{1,0:T(1,128)S(1)}, s32[1,128]{1,0:T(1,128)}, u32[]{:S(2)}) copy-start(s32[1,128]{1,0:T(1,128)} %param.41) | copy-start | bytes 1540
  122.5 14.4 %copy-start.15 = (f32[128,7,128]{0,2,1:T(8,128)S(1)}, f32[128,7,128]{0,2,1:T(8,128)}, u32[]{:S(2)}) copy-start(f32[128,7,128]{0,2,1:T(8,128)} %slice_convert_fusion.2) | copy-start | bytes 1376260
  126.3 12.9 %copy-start.12 = (f32[128,9,128]{0,2,1:T(8,128)S(1)}, f32[128,9,128]{0,2,1:T(8,128)}, u32[]{:S(2)}) copy-start(f32[128,9,128]{0,2,1:T(8,128)} %slice_convert_fusion) | copy-start | bytes 1769476
  137.5 22.5 %copy-start.14 = (f32[128,7,128]{0,2,1:T(8,128)S(1)}, f32[128,7,128]{0,2,1:T(8,128)}, u32[]{:S(2)}) copy-start(f32[128,7,128]{0,2,1:T(8,128)} %slice_convert_fusion.3) | copy-start | bytes 1376260
  160.8 11.8 %copy-start.55 = (f32[128,128]{1,0:T(8,128)S(1)}, f32[128,128]{1,0:T(8,128)}, u32[]{:S(2)}) copy-start(f32[128,128]{1,0:T(8,128)} %copy.488) | copy-start | bytes 196612
  160.8 11.8 %copy-start.56 = (f32[128,128]{1,0:T(8,128)S(1)}, f32[128,128]{1,0:T(8,128)}, u32[]{:S(2)}) copy-start(f32[128,128]{1,0:T(8,128)} %copy.490) | copy-start | bytes 196612
  160.8 11.8 %copy-start.57 = (f32[128,128]{1,0:T(8,128)S(1)}, f32[128,128]{1,0:T(8,128)}, u32[]{:S(2)}) copy-start(f32[128,128]{1,0:T(8,128)} %copy.489) | copy-start | bytes 196612
  162.2 11.3 %copy-start.65 = (f32[128,128]{1,0:T(8,128)S(1)}, f32[128,128]{1,0:T(8,128)}, u32[]{:S(2)}) copy-start(f32[128,128]{1,0:T(8,128)} %copy.491) | copy-start | bytes 196612
  162.3 11.3 %copy-start.66 = (f32[128,128]{1,0:T(8,128)S(1)}, f32[128,128]{1,0:T(8,128)}, u32[]{:S(2)}) copy-start(f32[128,128]{1,0:T(8,128)} %copy.495) | copy-start | bytes 196612
  162.3 11.3 %copy-start.67 = (f32[128,128]{1,0:T(8,128)S(1)}, f32[128,128]{1,0:T(8,128)}, u32[]{:S(2)}) copy-start(f32[128,128]{1,0:T(8,128)} %copy.494) | copy-start | bytes 196612
  162.3 11.3 %copy-start.68 = (f32[128,128]{1,0:T(8,128)S(1)}, f32[128,128]{1,0:T(8,128)}, u32[]{:S(2)}) copy-start(f32[128,128]{1,0:T(8,128)} %copy.493) | copy-start | bytes 196612
  162.3 11.3 %copy-start.69 = (f32[128,128]{1,0:T(8,128)S(1)}, f32[128,128]{1,0:T(8,128)}, u32[]{:S(2)}) copy-start(f32[128,128]{1,0:T(8,128)} %copy.492) | copy-start | bytes 196612
  165.2 9.7 %copy-start.71 = (f32[128,128]{1,0:T(8,128)S(1)}, f32[128,128]{1,0:T(8,128)}, u32[]{:S(2)}) copy-start(f32[128,128]{1,0:T(8,128)} %copy.496) | copy-start | bytes 196612
  165.2 9.7 %copy-start.78 = (f32[128,128]{1,0:T(8,128)S(1)}, f32[128,128]{1,0:T(8,128)}, u32[]{:S(2)}) copy-start(f32[128,128]{1,0:T(8,128)} %copy.502) | copy-start | bytes 196612
  165.2 9.7 %copy-start.79 = (f32[128,128]{1,0:T(8,128)S(1)}, f32[128,128]{1,0:T(8,128)}, u32[]{:S(2)}) copy-start(f32[128,128]{1,0:T(8,128)} %copy.501) | copy-start | bytes 196612
  180.3 10.6 %copy-start.1 = (bf16[2,384,384]{2,1,0:T(8,128)(2,1)S(1)}, bf16[2,384,384]{2,1,0:T(8,128)(2,1)}, u32[]{:S(2)}) copy-start(bf16[2,384,384]{2,1,0:T(8,128)(2,1)} %param.49) | copy-start | bytes 1769476
  185.5 11.9 %copy-start = (bf16[2,512,512]{2,1,0:T(8,128)(2,1)S(1)}, bf16[2,512,512]{2,1,0:T(8,128)(2,1)}, u32[]{:S(2)}) copy-start(bf16[2,512,512]{2,1,0:T(8,128)(2,1)} %param.48) | copy-start | bytes 3145732
  204.5 5.0 copy-start.35
  205.3 6.5 copy-start.34
  211.7 9.6 %copy-start.11 = (bf16[128,3,128]{0,2,1:T(8,128)(2,1)S(1)}, bf16[128,3,128]{0,2,1:T(8,128)(2,1)}, u32[]{:S(2)}) copy-start(bf16[128,3,128]{0,2,1:T(8,128)(2,1)} %copy.522) | copy-start | bytes 294916
  215.3 7.1 %copy-start.10 = (bf16[128,3,128]{0,2,1:T(8,128)(2,1)S(1)}, bf16[128,3,128]{0,2,1:T(8,128)(2,1)}, u32[]{:S(2)}) copy-start(bf16[128,3,128]{0,2,1:T(8,128)(2,1)} %copy.523) | copy-start | bytes 294916
  225.0 7.1 %copy-start.20 = (f32[128,512]{1,0:T(8,128)S(1)}, f32[128,512]{1,0:T(8,128)}, u32[]{:S(2)}) copy-start(f32[128,512]{1,0:T(8,128)} %fusion.14) | copy-start | bytes 786436
  226.3 7.9 %copy-start.100 = (bf16[128,1,128]{0,2,1:T(8,128)(2,1)S(1)}, bf16[128,1,128]{0,2,1:T(8,128)(2,1)}, u32[]{:S(2)}) copy-start(bf16[128,1,128]{0,2,1:T(8,128)(2,1)} %get-tuple-element.215) | copy-start | bytes 98308
  226.3 10.2 %copy-start.49 = (f32[128,1,128]{0,2,1:T(8,128)S(1)}, f32[128,1,128]{0,2,1:T(8,128)}, u32[]{:S(2)}) copy-start(f32[128,1,128]{0,2,1:T(8,128)} %get-tuple-element.218) | copy-start | bytes 196612
  227.3 12.3 %copy-start.32 = (f32[128,1,128]{0,2,1:T(8,128)S(1)}, f32[128,1,128]{0,2,1:T(8,128)}, u32[]{:S(2)}) copy-start(f32[128,1,128]{0,2,1:T(8,128)} %get-tuple-element.221) | copy-start | bytes 196612
  227.3 12.3 %copy-start.33 = (f32[128,128]{0,1:T(8,128)S(1)}, f32[128,128]{0,1:T(8,128)}, u32[]{:S(2)}) copy-start(f32[128,128]{0,1:T(8,128)} %get-tuple-element.229) | copy-start | bytes 196612
  252.0 12.6 %copy-start.18 = (bf16[5,128,128]{2,1,0:T(8,128)(2,1)S(1)}, bf16[5,128,128]{2,1,0:T(8,128)(2,1)}, u32[]{:S(2)}) copy-start(bf16[5,128,128]{2,1,0:T(8,128)(2,1)} %gather_fusion) | copy-start | bytes 491524
  253.4 12.0 %copy-start.27 = (bf16[4,128,128]{2,1,0:T(8,128)(2,1)S(1)}, bf16[4,128,128]{2,1,0:T(8,128)(2,1)}, u32[]{:S(2)}) copy-start(bf16[4,128,128]{2,1,0:T(8,128)(2,1)} %gather_fusion.1) | copy-start | bytes 393220
  265.6 7.6 %copy-start.6 = (bf16[128,4,128]{0,2,1:T(8,128)(2,1)}, bf16[128,4,128]{0,2,1:T(8,128)(2,1)S(1)}, u32[]{:S(2)}) copy-start(bf16[128,4,128]{0,2,1:T(8,128)(2,1)S(1)} %copy.457) | copy-start | bytes 393220
  267.6 5.6 copy-start.19
  275.0 5.7 copy-start.103
  275.0 8.0 %copy-start.31 = (bf16[128,384]{0,1:T(8,128)(2,1)S(1)}, bf16[128,384]{0,1:T(8,128)(2,1)}, u32[]{:S(2)}) copy-start(bf16[128,384]{0,1:T(8,128)(2,1)} %copy.467) | copy-start | bytes 294916
  276.4 7.3 %copy-start.30 = (bf16[128,9,128]{2,0,1:T(8,128)(2,1)S(1)}, bf16[128,9,128]{2,0,1:T(8,128)(2,1)}, u32[]{:S(2)}) copy-start(bf16[128,9,128]{2,0,1:T(8,128)(2,1)} %constant_dynamic-update-slice_fusion.20) | copy-start | bytes 884740
  276.4 7.3 %copy-start.101 = (bf16[128,1,128]{2,0,1:T(8,128)(2,1)S(1)}, bf16[128,1,128]{2,0,1:T(8,128)(2,1)}, u32[]{:S(2)}) copy-start(bf16[128,1,128]{2,0,1:T(8,128)(2,1)} %copy.480) | copy-start | bytes 98308
  276.4 7.3 %copy-start.102 = (bf16[128,1,128]{2,0,1:T(8,128)(2,1)S(1)}, bf16[128,1,128]{2,0,1:T(8,128)(2,1)}, u32[]{:S(2)}) copy-start(bf16[128,1,128]{2,0,1:T(8,128)(2,1)} %copy.481) | copy-start | bytes 98308
  285.5 6.0 copy-start.99
  290.6 10.9 %copy-start.3 = (f32[512,512]{1,0:T(8,128)S(1)}, f32[512,512]{1,0:T(8,128)}, u32[]{:S(2)}) copy-start(f32[512,512]{1,0:T(8,128)} %fusion.96) | copy-start | bytes 3145732
  292.2 10.5 %copy-start.2 = (f32[512,512]{1,0:T(8,128)S(1)}, f32[512,512]{1,0:T(8,128)}, u32[]{:S(2)}) copy-start(f32[512,512]{1,0:T(8,128)} %fusion.95) | copy-start | bytes 3145732
  315.2 5.3 copy-start.80
  315.2 380.5 %all-reduce.8.cloned.1.call-start = ((), (), s32[]{:S(2)}) async-start(), calls=%async_computation.3 | async-start | bytes 6553600
  315.3 5.2 copy-start.81
  315.3 5.2 copy-start.82
  315.3 5.2 copy-start.83
  315.3 5.2 copy-start.84
  315.3 5.2 copy-start.85
  315.3 5.2 copy-start.86
  315.3 5.2 copy-start.87
  315.4 5.2 copy-start.88
  318.2 5.4 copy-start.24
  318.3 5.4 copy-start.50
  318.3 5.5 copy-start.51
  318.3 5.5 copy-start.52
  (80 other events, 179.0 us)
Sparse Core Ops, SparseCore 0:
  10.4 51.8 all-gather.6
  64.8 48.6 all-gather.4
  315.3 270.5 all-reduce.5
  589.1 106.6 all-reduce.7
where the time goes:
time: 709 us; the launch traced here: 705 us
  waiting for transfers between devices  433 us (61%)
  local copies, waits for them, and re-layouts  179 us (25%)
  other arithmetic  44.5 us (6%)
  matrix products  31.6 us (4%)
  between operations  17.3 us (2%)
    psum x1, waiting for transfers between devices, per_device(): summed = lax.psum(flat, ('dp', 'graph'))  251 us
    unnamed x5, waiting for transfers between devices  103 us
    mul x65, local copies, waits for them, and re-layouts, rotate_blocks(): total = total + block[:, :, inner, None] * coef_piece[:, None, inner, :]  63.8 us
    all_gather x1, waiting for transfers between devices, per_device(): lax.all_gather(node_feats[0], 'graph', axis=0, tiled=True)  47.6 us
    all_gather x1, waiting for transfers between devices, per_device(): lax.all_gather(cotangent[0], 'graph', axis=0, tiled=True)  30.9 us
    mul x35, local copies, waits for them, and re-layouts, rotate_blocks(): total = block[:, :, 0, None] * coef_piece[:, None, 0, :]  26.6 us
    unnamed x308, local copies, waits for them, and re-layouts  20.4 us
    gather x20, local copies, waits for them, and re-layouts, pick_rows(): values[:, np.array(indices), :]  16.7 us
  transfers between devices with their start and end apart: 4, of which 4 were waited for; matrix products, arithmetic and copies ran while one was open for 6% of the time, Pallas kernels for 0%

commit v1 on v0

v1 whole, which is shorter than its diff:
```python
import functools, math
import jax, jax.numpy as jnp, numpy as np
from jax import lax
from jax.experimental import pallas as pl
from jax.experimental.pallas import tpu as pltpu
from jax.sharding import PartitionSpec as P

C = 128
E = 128
N = 256
W = 25 * C
F32, BF16 = jnp.float32, jnp.bfloat16
OFF = [0, 1, 10, 35, 84]


def dot(a, b):
    return lax.dot_general(a, b, (((1,), (0,)), ((), ())), preferred_element_type=F32)


def dot_nt(a, b):
    return lax.dot_general(a, b, (((1,), (1,)), ((), ())), preferred_element_type=F32)


def dot_tn(a, b):
    return lax.dot_general(a, b, (((0,), (0,)), ((), ())), preferred_element_type=F32)


def orders(l):
    top = min(l, 2)
    return range(-top, top + 1)


def kept(l):
    return sum(len(orders(q)) * (2 * q + 1) for q in range(l))


def prepare(src, dst, count, rot, oh_s, oh_d, oh_st, oh_dt, rot_t):
    node = lax.broadcasted_iota(jnp.int32, (N, E), 0)
    slot = lax.broadcasted_iota(jnp.int32, (N, E), 1)
    s = (node == src).astype(F32)
    d = ((node == dst) & (slot < count)).astype(F32)
    oh_st[...] = s.astype(BF16)
    oh_dt[...] = d.astype(BF16)
    oh_s[...] = s.T.astype(BF16)
    oh_d[...] = d.T.astype(BF16)
    eye = (lax.broadcasted_iota(jnp.int32, (E, E), 0) == lax.broadcasted_iota(jnp.int32, (E, E), 1)).astype(BF16)
    k = lax.broadcasted_iota(jnp.int32, (1, 165), 1)
    scale = jnp.ones((1, 165), F32)
    for l in range(1, 5):
        scale = jnp.where(k >= OFF[l], 1.0 / math.sqrt(2 * l + 1), scale)
    rot_t[:, :165] = dot_nt(eye, rot) * scale


def group_slot(l, m):
    return abs(m), (E if m < 0 else 0), (l - abs(m)) * C


def rotate_in(l, feats, cots, oh_s, oh_d, rad, rot_t, x_buf, u_buf, wide, act, ups, ups_s):
    size = 2 * l + 1
    x_buf[:, : size * C] = dot(oh_s[...], feats)
    u_buf[:, : size * C] = dot(oh_d[...], cots)

    @pl.loop(0, E // 16)
    def _(b):
        r = pl.multiple_of(b * 16, 16)
        rows = pl.ds(r, 16)
        rt = rot_t[rows, :]
        xs = [x_buf[rows, j * C : (j + 1) * C] for j in range(size)]
        us = [u_buf[rows, j * C : (j + 1) * C] for j in range(size)]
        rd = rad[rows, l * C : (l + 1) * C].astype(F32)
        at = kept(l)
        for m in orders(l):
            a = u = None
            for j in range(size):
                k = OFF[l] + (m + l) * size + j
                w = jnp.broadcast_to(rt[:, k : k + 1], (16, C))
                wide[at, rows, :] = w
                at += 1
                a = w * xs[j] if a is None else a + w * xs[j]
                u = w * us[j] if u is None else u + w * us[j]
            g, ro, co = group_slot(l, m)
            here = pl.ds(r + ro, 16)
            cols = slice(co, co + C)
            act[g][here, cols] = (a * rd).astype(BF16)
            ub = u.astype(BF16)
            ups[g][here, cols] = ub
            if g:
                there = pl.ds(r + E - ro, 16)
                ups_s[g][there, cols] = ub if m < 0 else -ub


def plane(act, ups, ws, msg, back):
    msg[0][...] = dot(act[0][...], ws[0][...])
    back[0][...] = dot_nt(ups[0][...], ws[0][...])
    for g in (1, 2):
        a = act[g][...]
        y0 = dot(a, ws[g][0])
        y1 = dot(a, ws[g][1])
        msg[g][:E, :] = y0[:E] - y1[E:]
        msg[g][E:, :] = y0[E:] + y1[:E]
        u = ups[g][...]
        z0 = dot_nt(u, ws[g][0])
        z1 = dot_nt(u, ws[g][1])
        back[g][:E, :] = z0[:E] + z1[E:]
        back[g][E:, :] = z0[E:] - z1[:E]


def rotate_out(l, msg, back, rad, wide, oh_st, oh_dt, m_buf, e_buf, out, grad):
    size = 2 * l + 1

    @pl.loop(0, E // 16)
    def _(b):
        r = pl.multiple_of(b * 16, 16)
        rows = pl.ds(r, 16)
        rd = rad[rows, l * C : (l + 1) * C].astype(F32)
        ms, bs = [], []
        for m in orders(l):
            g, ro, co = group_slot(l, m)
            here = pl.ds(r + ro, 16)
            ms.append(msg[g][here, co : co + C])
            bs.append(back[g][here, co : co + C] * rd)
        n = len(ms)
        for i in range(size):
            a = u = None
            for j in range(n):
                w = wide[kept(l) + j * size + i, rows, :]
                a = w * ms[j] if a is None else a + w * ms[j]
                u = w * bs[j] if u is None else u + w * bs[j]
            m_buf[rows, i * C : (i + 1) * C] = a.astype(BF16)
            e_buf[rows, i * C : (i + 1) * C] = u.astype(BF16)

    cols = slice(l * l * C, (l + 1) * (l + 1) * C)
    out[:, cols] = dot(oh_dt[...], m_buf[:, : size * C]).astype(BF16)
    grad[:, cols] = dot(oh_st[...], e_buf[:, : size * C]).astype(BF16)


def weight_grads(act, ups, ups_s, flat):
    scale = 1.0 / math.sqrt(32768)
    at = 0
    for g in range(3):
        left = act[g][...].T
        for right in (ups, ups_s)[: 1 if g == 0 else 2]:
            total = (dot(left, right[g][...]) * scale).astype(BF16)
            rows = total.shape[0]
            for c in range(rows // C):
                flat[at : at + rows // 16] = total[:, c * C : (c + 1) * C].reshape(rows // 16, 16, C)
                at += rows // 16
    flat[600:608] = jnp.zeros((8, 16, C), BF16)


def compute_kernel(count, src, dst, rot, rad, feats, cots, w0, w1, w2, out, grad, flat,
                   oh_s, oh_d, oh_st, oh_dt, rot_t, x_buf, u_buf, wide, a0, a1, a2, u0, u1, u2, v1, v2,
                   m0, m1, m2, b0, b1, b2, mb, eb):
    prepare(src[...], dst[...], count[0, 0], rot[...], oh_s, oh_d, oh_st, oh_dt, rot_t)
    act, ups, ups_s = (a0, a1, a2), (u0, u1, u2), (None, v1, v2)
    ws, msg, back = (w0, w1, w2), (m0, m1, m2), (b0, b1, b2)
    for l in range(5):
        cols = slice(l * l * C, (l + 1) * (l + 1) * C)
        rotate_in(l, feats[:, cols], cots[:, cols], oh_s, oh_d, rad, rot_t, x_buf, u_buf, wide, act, ups, ups_s)
    weight_grads(act, ups, ups_s, flat)
    plane(act, ups, ws, msg, back)
    for l in range(5):
        rotate_out(l, msg, back, rad, wide, oh_st, oh_dt, mb, eb, out, grad)


def compute(count, src, dst, rot, rad, feats, cots, w0, w1, w2):
    v = pl.BlockSpec(memory_space=pltpu.VMEM)
    V = pltpu.VMEM
    return pl.pallas_call(
        compute_kernel,
        out_shape=(
            jax.ShapeDtypeStruct((N, W), BF16), jax.ShapeDtypeStruct((N, W), BF16),
            jax.ShapeDtypeStruct((608, 16, C), BF16)),
        in_specs=[pl.BlockSpec(memory_space=pltpu.SMEM)] + [v] * 9,
        out_specs=(v,) * 3,
        scratch_shapes=[
            V((E, N), BF16), V((E, N), BF16), V((N, E), BF16), V((N, E), BF16), V((E, 256), F32),
            V((E, 9 * C), F32), V((E, 9 * C), F32), V((115, E, C), F32),
            V((E, 640), BF16), V((2 * E, 512), BF16), V((2 * E, 384), BF16),
            V((E, 640), BF16), V((2 * E, 512), BF16), V((2 * E, 384), BF16),
            V((2 * E, 512), BF16), V((2 * E, 384), BF16),
            V((E, 640), F32), V((2 * E, 512), F32), V((2 * E, 384), F32),
            V((E, 640), F32), V((2 * E, 512), F32), V((2 * E, 384), F32),
            V((E, 9 * C), BF16), V((E, 9 * C), BF16),
        ],
        compiler_params=pltpu.CompilerParams(vmem_limit_bytes=56 * 2**20),
        name="edge_block",
    )(count, src, dst, rot, rad, feats, cots, w0, w1, w2)

MESH = pl.DeviceIdType.MESH
TILES = 304
PIECE = 38


def start_at(g):
    return lax.div(g * 35, 15) if not isinstance(g, int) else g * 35 // 15


def wrap(p, d, n):
    return lax.rem(p + (d % n), n)


class Place:
    def __init__(self):
        g, p = lax.axis_index("graph"), lax.axis_index("dp")
        self.g, self.p = g, p
        self.y, self.x = lax.div(g, 4), lax.rem(g, 4)
        self.z, self.c = lax.div(p, 2), lax.rem(p, 2)

    def plane(self, dy, dx):
        return (self.p, wrap(self.y, dy, 4) * 4 + wrap(self.x, dx, 4))

    def peer(self, d):
        return (self.p, wrap(self.g, d, 16))

    def up(self, d):
        return (wrap(self.z, d, 8) * 2 + self.c, self.g)

    def sibling(self):
        return (self.z * 2 + 1 - self.c, self.g)


def greet(devices):
    barrier = pltpu.get_barrier_semaphore()
    for d in devices:
        pl.semaphore_signal(barrier, inc=1, device_id=d, device_id_type=MESH)
    pl.semaphore_wait(barrier, len(devices))


class Sender:
    def __init__(self, send, recv):
        self.send, self.recv, self.next, self.all = send, recv, 0, []

    def make(self, src, dst, to):
        k = self.next
        self.next += 1
        c = pltpu.make_async_remote_copy(src_ref=src, dst_ref=dst, send_sem=self.send.at[k], recv_sem=self.recv.at[k],
                                         device_id=to, device_id_type=MESH)
        self.all.append(c)
        return c

    def go(self, src, dst, to):
        c = self.make(src, dst, to)
        c.start()
        return c

    def finish(self):
        for c in self.all:
            c.wait_send()


def interleave(streams):
    streams = list(streams)
    while streams:
        left = []
        for s in streams:
            try:
                next(s)
                left.append(s)
            except StopIteration:
                pass
        streams = left


def gather_stream(snd, at, dev, done=lambda da, db: None):
    def spread(da):
        return [snd.go(at(da, 0, None), at(da, 0, None), dev(0, s)) for s in (1, -1)]

    def relay(da, got):
        for k, s in enumerate((1, -1)):
            yield
            got[k].wait_recv()
            done(da, -s)
            last.append(snd.go(at(da, -s, k), at(da, -s, k), dev(0, s)))

    last = []
    first = [snd.go(at(0, 0, None), at(0, 0, None), dev(s, 0)) for s in (1, -1)]
    second = {0: spread(0)}
    done(0, 0)
    far = []
    for k, s in enumerate((1, -1)):
        yield
        first[k].wait_recv()
        far.append(snd.go(at(-s, 0, k), at(-s, 0, k), dev(s, 0)))
        second[-s] = spread(-s)
        done(-s, 0)
    yield from relay(0, second[0])
    yield
    for f in far:
        f.wait_recv()
    second[2] = spread(2)
    done(2, 0)
    for da in (-1, 1, 2):
        yield from relay(da, second[da])
    for i, da in enumerate((0, -1, 1, 2)):
        yield
        last[2 * i].wait_recv()
        last[2 * i + 1].wait_recv()
        done(da, 2)


CHUNKS = ((0, 9), (9, 16), (16, 25))


def col_at(buf, pl_, lo, hi, y_first):
    mid = (lo + hi) // 2
    parts = {None: (lo, hi), 0: (lo, mid), 1: (mid, hi)}

    def at(da, db, part):
        dy, dx = (da, db) if y_first else (db, da)
        a, b = parts[part]
        return buf.at[wrap(pl_.y, dy, 4), wrap(pl_.x, dx, 4), :, a * C : b * C]
    return at


def plane_dev(pl_, y_first):
    return (lambda da, db: pl_.plane(da, db)) if y_first else (lambda da, db: pl_.plane(db, da))


def gather_kernel(chunks, f_in, c_in, f_out, c_out, send, recv):
    here = Place()
    greet([here.plane(*d) for d in ((0, 1), (0, -1), (1, 0), (-1, 0))])
    f_out[here.y, here.x] = f_in[0]
    c_out[here.y, here.x] = c_in[0]
    snd = Sender(send, recv)
    streams = []
    for lo, hi in chunks:
        for buf, yf in ((f_out, False), (c_out, True)):
            streams.append(gather_stream(snd, col_at(buf, here, lo, hi, yf), plane_dev(here, yf)))
    interleave(streams)
    snd.finish()


def gather(feats, cots, chunks=CHUNKS):
    v = pl.BlockSpec(memory_space=pltpu.VMEM)
    n = 20 * 2 * len(chunks)
    o = jax.ShapeDtypeStruct((4, 4, 16, W), BF16)
    f, c = pl.pallas_call(
        functools.partial(gather_kernel, chunks),
        out_shape=(o, o), in_specs=[v, v], out_specs=(v, v),
        scratch_shapes=[pltpu.SemaphoreType.DMA((n,)), pltpu.SemaphoreType.DMA((n,))],
        compiler_params=pltpu.CompilerParams(collective_id=0, has_side_effects=True, vmem_limit_bytes=32 * 2**20),
        name="gather_nodes",
    )(feats, cots)
    return f.reshape(N, W), c.reshape(N, W)


def add(*xs):
    t = xs[0].astype(F32)
    for x in xs[1:]:
        t = t + x.astype(F32)
    return t.astype(BF16)


def scatter_stream(snd, part, mid, t, r, q, t2, r2, out, here, lo, hi, y_first):
    cm = (lo + hi) // 2
    full, halves = slice(lo * C, hi * C), (slice(lo * C, cm * C), slice(cm * C, hi * C))
    a, b = (here.y, here.x) if y_first else (here.x, here.y)
    dev = plane_dev(here, y_first)

    def row(da, cols):
        i = wrap(a, da, 4)
        return part.at[i, :, :, cols] if y_first else part.at[:, i, :, cols]

    got = [snd.go(row(2, halves[k]), t.at[k, :, :, halves[k]], dev(s, 0)) for k, s in enumerate((1, -1))]
    sent = []
    for k, s in enumerate((1, -1)):
        yield
        got[k].wait_recv()
        mid[k, :, :, halves[k]] = add(row(s, halves[k])[...], t[k, :, :, halves[k]])
        mid[k, :, :, halves[1 - k]] = row(s, halves[1 - k])[...]
        sent.append(snd.go(mid.at[k, :, :, full], r.at[k, :, :, full], dev(s, 0)))
    yield
    sent[0].wait_recv()
    sent[1].wait_recv()
    q[:, :, full] = add(row(0, full)[...], r[0, :, :, full], r[1, :, :, full])
    far = wrap(b, 2, 4)
    got = [snd.go(q.at[far, :, halves[k]], t2.at[k, :, halves[k]], dev(0, s)) for k, s in enumerate((1, -1))]
    sent = []
    for k, s in enumerate((1, -1)):
        yield
        got[k].wait_recv()
        i = wrap(b, s, 4)
        q[i, :, halves[k]] = add(q[i, :, halves[k]], t2[k, :, halves[k]])
        sent.append(snd.go(q.at[i, :, full], r2.at[k, :, full], dev(0, s)))
    yield
    sent[0].wait_recv()
    sent[1].wait_recv()
    out[0, :, full] = add(q[b, :, full], r2[0, :, full], r2[1, :, full])


def swap_cores(snd, flat, sib, here):
    other = (1 - here.c) * TILES
    copies = {}
    for d in (-1, 1, -2, 2, -3, 3, 4, 0):
        k = wrap(here.z, d, 8) * PIECE
        copies[d % 8] = snd.go(flat.at[pl.ds(other + k, PIECE)], sib.at[pl.ds(k, PIECE)], here.sibling())
    return copies


def z_stream(snd, copies, seen, flat, sib, box, outbox, zsum, here, sign, lo, hi):
    def mine(d):
        if d not in seen:
            seen.add(d)
            copies[d].wait_recv()
        k = wrap(here.z, d, 8) * PIECE + lo
        return flat[pl.ds(here.c * TILES + k, hi - lo)], sib[pl.ds(k, hi - lo)]

    got = None
    for s in range(7):
        yield
        terms = mine((-sign * (1 + s)) % 8)
        if got is not None:
            got.wait_recv()
            terms += (box[s - 1, lo:hi],)
        outbox[s, lo:hi] = add(*terms)
        got = snd.go(outbox.at[s, lo:hi], box.at[s, lo:hi], here.up(sign))
    yield
    terms = mine(0)
    got.wait_recv()
    zsum[lo:hi] = add(*terms, box[6, lo:hi])


def plane_sum(snd, zsum, xbox, g_buf, here):
    copies = []
    for d in range(1, 16):
        to = wrap(here.g, d, 16)
        copies.append(snd.go(zsum.at[pl.ds(start_at(to), 3)], xbox.at[d], here.peer(d)))
    total = zsum[pl.ds(start_at(here.g), 3)].astype(F32)
    for d in range(1, 16):
        copies[d - 1].wait_recv()
        total = total + xbox[d].astype(F32)
    g_buf[here.y, here.x, here.z] = total.astype(BF16)
    own = g_buf.at[here.y, here.x, here.z]
    return [snd.go(own, own, here.up(d)) for d in range(1, 8)]


def z_at(buf, here, lo, hi, y_first):
    mid = (lo + hi) // 2
    parts = {None: (lo, hi), 0: (lo, mid), 1: (mid, hi)}

    def at(da, db, part):
        dy, dx = (da, db) if y_first else (db, da)
        a, b = parts[part]
        return buf.at[wrap(here.y, dy, 4), wrap(here.x, dx, 4), a:b]
    return at


def weight_out(snd, g_buf, g_sib, here):
    cores = []
    streams = []
    for lo, hi, yf in ((0, 4, False), (4, 8, True)):
        at = z_at(g_buf, here, lo, hi, yf)
        to = z_at(g_sib, here, lo, hi, yf)
        streams.append(gather_stream(
            snd, at, plane_dev(here, yf),
            lambda da, db, at=at, to=to: cores.append(snd.go(at(da, db, None), to(da, db, None), here.sibling()))))
    interleave(streams)
    for c in cores:
        c.wait_recv()


def unpack(g_buf, g_sib, flat, here, g0, g1, g2):
    for buf, base in ((g_buf, here.c * TILES), (g_sib, (1 - here.c) * TILES)):
        for g in range(16):
            for z in range(8):
                flat[pl.ds(base + (z * PIECE + start_at(g)), 3)] = buf[g // 4, g % 4, z]
    for c in range(5):
        g0[:, c * C : (c + 1) * C] = flat[c * 40 : c * 40 + 40].reshape(640, C).astype(F32)
    for i in range(2):
        for c in range(4):
            b = 200 + i * 128 + c * 32
            g1[i, :, c * C : (c + 1) * C] = flat[b : b + 32].reshape(512, C).astype(F32)
        for c in range(3):
            b = 456 + i * 72 + c * 24
            g2[i, :, c * C : (c + 1) * C] = flat[b : b + 24].reshape(384, C).astype(F32)


Z_STREAMS = ((1, 0, 10), (-1, 19, 29), (1, 10, 19), (-1, 29, 38))


def all_partners(here):
    return [here.sibling()] + [here.up(d) for d in range(1, 8)] + [here.peer(d) for d in range(1, 16)]


RCHUNKS = ((0, 9), (9, 16), (16, 25))


def reduce_kernel(chunks, p_out, p_grad, w_flat, out, grad, g0, g1, g2,
                  mid, t, r, q, t2, r2, sib, box, outbox, zsum, xbox, g_buf, g_sib, flat, send, recv):
    here = Place()
    greet(all_partners(here))
    snd = Sender(send, recv)
    copies = swap_cores(snd, w_flat, sib, here)
    seen = set()
    streams = [z_stream(snd, copies, seen, w_flat, sib, box, outbox, zsum, here, *z) for z in Z_STREAMS]
    for lo, hi in chunks:
        for i, (part, dst, yf) in enumerate(((p_out, out, True), (p_grad, grad, False))):
            streams.append(scatter_stream(snd, part, mid.at[i], t.at[i], r.at[i], q.at[i], t2.at[i], r2.at[i], dst, here, lo, hi, yf))
    interleave(streams)
    for c in plane_sum(snd, zsum, xbox, g_buf, here):
        c.wait_recv()
    weight_out(snd, g_buf, g_sib, here)
    snd.finish()
    unpack(g_buf, g_sib, flat, here, g0, g1, g2)


def reduce(p_out, p_grad, w_flat, chunks=RCHUNKS):
    v = pl.BlockSpec(memory_space=pltpu.VMEM)
    V = pltpu.VMEM
    n = 8 + 28 + 16 * len(chunks) + 15 + 7 + 2 * (20 + 16)
    o = jax.ShapeDtypeStruct((1, 16, W), BF16)
    return pl.pallas_call(
        functools.partial(reduce_kernel, chunks),
        out_shape=(o, o, jax.ShapeDtypeStruct((640, 640), F32), jax.ShapeDtypeStruct((2, 512, 512), F32),
                   jax.ShapeDtypeStruct((2, 384, 384), F32)),
        in_specs=[v] * 3, out_specs=(v,) * 5,
        scratch_shapes=[
            V((2, 2, 4, 16, W), BF16), V((2, 2, 4, 16, W), BF16), V((2, 2, 4, 16, W), BF16), V((2, 4, 16, W), BF16),
            V((2, 2, 16, W), BF16), V((2, 2, 16, W), BF16),
            V((TILES, 16, C), BF16), V((7, PIECE, 16, C), BF16), V((7, PIECE, 16, C), BF16), V((PIECE, 16, C), BF16),
            V((16, 3, 16, C), BF16), V((4, 4, 8, 3, 16, C), BF16), V((4, 4, 8, 3, 16, C), BF16), V((2 * TILES, 16, C), BF16),
            pltpu.SemaphoreType.DMA((n,)), pltpu.SemaphoreType.DMA((n,))],
        compiler_params=pltpu.CompilerParams(collective_id=1, has_side_effects=True, vmem_limit_bytes=56 * 2**20),
        name="reduce_all",
    )(p_out.reshape(4, 4, 16, W), p_grad.reshape(4, 4, 16, W), w_flat)


def per_device(node_feats, source, target, rotation, radial, edge_count, cotangent, weight_zero, weight_first, weight_second):
    feats, cots = gather(node_feats, cotangent)
    p_out, p_grad, flat = compute(
        edge_count, source, target, rotation[0], radial[0], feats, cots, weight_zero, weight_first, weight_second)
    return tuple(reduce(p_out, p_grad, flat))


def solution(mesh):
    edge = P("dp", "graph")
    node = P("dp", "graph", None)
    return jax.shard_map(
        per_device,
        mesh=mesh,
        in_specs=(node, edge, edge, P("dp", None, "graph"), node, edge, node, P(), P(), P()),
        out_specs=(node, node, P(), P(), P()),
        check_vma=False,
    )
```

time: 709 us -> 135 us (0.19)
  waiting for transfers between devices: 433 us -> 0 us
  local copies, waits for them, and re-layouts: 179 us -> 13.1 us
  Pallas kernels: 0 us -> 120 us
  other arithmetic: 44.5 us -> 0 us
  matrix products: 31.6 us -> 0 us
  between operations: 17.3 us -> 1.32 us
    psum x1 -> x0, waiting for transfers between devices: 251 us -> none  [per_device(): summed = lax.psum(flat, ('dp', 'graph'))]
    pallas_call x0 -> x3, Pallas kernels: none -> 120 us  [the longest x1 78.9 us: reduce(): pl.pallas_call(functools.partial(reduce_kernel, chunks), out_shape=(o, o,...]
    unnamed x5 -> x0, waiting for transfers between devices: 103 us -> none
    mul x105 -> x0, local copies, waits for them, and re-layouts: 94.8 us -> none  [the longest x65 63.8 us: rotate_blocks(): total = total + block[:, :, inner, None] * coef_piece[:, None, inner, :]]
    all_gather x2 -> x0, waiting for transfers between devices: 78.5 us -> none  [the longest x1 47.6 us: per_device(): lax.all_gather(node_feats[0], 'graph', axis=0, tiled=True)]
    dot_general x31 -> x0, matrix products: 31.6 us -> none  [the longest x11 11.2 us: contract_rows(): lax.dot_general(left, right, (((0,), (0,)), ((), ())), preferred_element_...]
    slice x34 -> x0, local copies, waits for them, and re-layouts: 21.7 us -> none  [the longest x19 15.8 us: join_groups(): columns[coef_index] = shaped[:, position, :]]
    gather x20 -> x0, local copies, waits for them, and re-layouts: 16.7 us -> none  [pick_rows(): values[:, np.array(indices), :]]
  transfers between devices with their start and end apart: 4 -> 0, of which waited for: 4 -> 0; matrix products, arithmetic and copies ran while one was open for 6% -> 0% of each run, Pallas kernels for 0% -> 0%
where the time goes in v1:
time: 135 us
  Pallas kernels  120 us (89%)
  local copies, waits for them, and re-layouts  13.1 us (10%)
    pallas_call x1, Pallas kernels, reduce(): pl.pallas_call(functools.partial(reduce_kernel, chunks), out_shape=(o, o,...  78.9 us
    pallas_call x1, Pallas kernels, gather(): pl.pallas_call(functools.partial(gather_kernel, chunks), out_shape=(o, o)...  23.9 us
    pallas_call x1, Pallas kernels, compute(): pl.pallas_call(compute_kernel, out_shape=(jax.ShapeDtypeStruct((N, W), BF...  17.6 us
    unnamed x17, local copies, waits for them, and re-layouts  13.1 us

profile of v1, /device:TPU:1, one launch (start us, length us, event | category | flops | bytes accessed | tf_op | source)
XLA Modules:
  0.0 134.8 jit_solution(17948349453085853012)
XLA Ops:
  1.3 0.0 copy-start.2
  1.3 0.9 copy-done.2
  2.2 0.0 copy-start.3
  2.2 0.9 copy-done.3
  3.1 23.9 %gather_nodes.1 = (bf16[4,4,16,3200]{3,2,1,0:T(8,128)(2,1)S(1)}, bf16[4,4,16,3200]{3,2,1,0:T(8,128)(2,1)S(1)}) custom-call(bf16[1,16,3200]{2,1,0:T(8,128)(2,1)S(1)} %copy-done.2, bf16[1,16,3200]{2,1,0:T(8,128)(2,1)S(1)} %copy-done.3), custom_call_target="tpu_custom_call" | custom-call | tf_op jit(solution)/shard_map/gather_nodes/pallas_call | solution.py:338
  26.9 0.0 copy-start
  26.9 1.2 copy-done
  28.1 0.0 copy-start.1
  28.1 1.2 copy-done.1
  29.3 17.6 %edge_block.1 = (bf16[256,3200]{1,0:T(8,128)(2,1)}, bf16[256,3200]{1,0:T(8,128)(2,1)}, bf16[608,16,128]{2,1,0:T(8,128)(2,1)}) custom-call(s32[1,1]{1,0:T(1,128)S(6)} %copy.20.count, s32[1,128]{1,0:T(1,128)} %src.1, s32[1,128]{1,0:T(1,128)} %dst.1, bf16[165,128]{1,0:T(8,128)(2,1)} %bitcast.11, bf16[128,640]{1,0:T(8,128)(2,1)} %bitcast.10, ...), custom_call_target="tpu_custom_call" | custom-call | tf_op jit(solution)/shard_map/edge_block/pallas_call | solution.py:169
  46.9 78.9 %reduce_all.1 = (bf16[1,16,3200]{2,1,0:T(8,128)(2,1)}, bf16[1,16,3200]{2,1,0:T(8,128)(2,1)}, f32[640,640]{1,0:T(8,128)}, f32[2,512,512]{2,1,0:T(8,128)}, f32[2,384,384]{2,1,0:T(8,128)}) custom-call(bf16[4,4,16,3200]{3,2,1,0:T(8,128)(2,1)} %bitcast.8, bf16[4,4,16,3200]{3,2,1,0:T(8,128)(2,1)} %bitcast.9, bf16[608,16,128]{2,1,0:T(8,128)(2,1)} %get-tuple-element.14.w_flat), custom_call_target="tpu_custom_call" | custom-call | tf_op jit(solution)/shard_map/reduce_all/pallas_call | solution.py:513
  125.8 1.5 %copy.21 = bf16[1,16,3200]{2,1,0:T(8,128)(2,1)} copy(bf16[1,16,3200]{2,1,0:T(8,128)(2,1)} %get-tuple-element.20) | data formatting | bytes 204800
  127.3 1.5 %copy.22 = bf16[1,16,3200]{2,1,0:T(8,128)(2,1)} copy(bf16[1,16,3200]{2,1,0:T(8,128)(2,1)} %get-tuple-element.21) | data formatting | bytes 204800
  128.9 0.0 copy-start.4
  128.9 2.8 %copy.23 = f32[640,640]{1,0:T(8,128)} copy(f32[640,640]{1,0:T(8,128)} %get-tuple-element.22) | data formatting | bytes 3276800
  131.7 0.0 copy-done.4
  131.7 0.0 copy-start.5
  131.7 1.3 copy.24
  133.0 0.7 copy-done.5
  133.7 1.0 copy.25
Async XLA Ops:
  1.3 0.9 copy-start.2
  2.2 0.9 copy-start.3
  26.9 1.2 copy-start
  28.1 1.2 copy-start.1
  128.9 2.9 %copy-start.4 = (f32[2,512,512]{2,1,0:T(8,128)S(1)}, f32[2,512,512]{2,1,0:T(8,128)}, u32[]{:S(2)}) copy-start(f32[2,512,512]{2,1,0:T(8,128)} %get-tuple-element.23) | copy-start | bytes 6291460
  131.7 2.0 %copy-start.5 = (f32[2,384,384]{2,1,0:T(8,128)S(1)}, f32[2,384,384]{2,1,0:T(8,128)}, u32[]{:S(2)}) copy-start(f32[2,384,384]{2,1,0:T(8,128)} %get-tuple-element.24) | copy-start | bytes 3538948

commit v2 on v1

v2 whole, which is shorter than its diff:
```python
import functools, math
import jax, jax.numpy as jnp, numpy as np
from jax import lax
from jax.experimental import pallas as pl
from jax.experimental.pallas import tpu as pltpu
from jax.sharding import PartitionSpec as P

C = 128
E = 128
N = 256
W = 25 * C
F32, BF16 = jnp.float32, jnp.bfloat16
OFF = [0, 1, 10, 35, 84]


def dot(a, b):
    return lax.dot_general(a, b, (((1,), (0,)), ((), ())), preferred_element_type=F32)


def dot_nt(a, b):
    return lax.dot_general(a, b, (((1,), (1,)), ((), ())), preferred_element_type=F32)


def dot_tn(a, b):
    return lax.dot_general(a, b, (((0,), (0,)), ((), ())), preferred_element_type=F32)


def orders(l):
    top = min(l, 2)
    return range(-top, top + 1)


def kept(l):
    return sum(len(orders(q)) * (2 * q + 1) for q in range(l))


def prepare(src, dst, count, rot, oh_s, oh_d, oh_st, oh_dt, rot_t):
    node = lax.broadcasted_iota(jnp.int32, (N, E), 0)
    slot = lax.broadcasted_iota(jnp.int32, (N, E), 1)
    s = (node == src).astype(F32)
    d = ((node == dst) & (slot < count)).astype(F32)
    oh_st[...] = s.astype(BF16)
    oh_dt[...] = d.astype(BF16)
    oh_s[...] = s.T.astype(BF16)
    oh_d[...] = d.T.astype(BF16)
    eye = (lax.broadcasted_iota(jnp.int32, (E, E), 0) == lax.broadcasted_iota(jnp.int32, (E, E), 1)).astype(BF16)
    k = lax.broadcasted_iota(jnp.int32, (1, 165), 1)
    scale = jnp.ones((1, 165), F32)
    for l in range(1, 5):
        scale = jnp.where(k >= OFF[l], 1.0 / math.sqrt(2 * l + 1), scale)
    rot_t[:, :165] = dot_nt(eye, rot) * scale


def group_slot(l, m):
    return abs(m), (E if m < 0 else 0), (l - abs(m)) * C


PARTS = (1, 1, 1, 2, 2)


def loop_parts(step, parts):
    for p in range(parts):
        if p:
            yield
        pl.loop(p * 8 // parts, (p + 1) * 8 // parts)(step)


def rotate_in(l, feats, cots, oh_s, oh_d, rad, rot_t, x_buf, u_buf, wide, act, ups, ups_s):
    size = 2 * l + 1
    cols = slice(l * l * C, (l + 1) * (l + 1) * C)
    x_buf[:, : size * C] = dot(oh_s[...], feats[:, :, :, cols].reshape(N, size * C))
    u_buf[:, : size * C] = dot(oh_d[...], cots[:, :, :, cols].reshape(N, size * C))

    def step(b):
        r = pl.multiple_of(b * 16, 16)
        rows = pl.ds(r, 16)
        rt = rot_t[rows, :]
        xs = [x_buf[rows, j * C : (j + 1) * C] for j in range(size)]
        us = [u_buf[rows, j * C : (j + 1) * C] for j in range(size)]
        rd = rad[rows, l * C : (l + 1) * C].astype(F32)
        at = kept(l)
        for m in orders(l):
            a = u = None
            for j in range(size):
                k = OFF[l] + (m + l) * size + j
                w = jnp.broadcast_to(rt[:, k : k + 1], (16, C))
                wide[at, rows, :] = w
                at += 1
                a = w * xs[j] if a is None else a + w * xs[j]
                u = w * us[j] if u is None else u + w * us[j]
            g, ro, co = group_slot(l, m)
            here = pl.ds(r + ro, 16)
            cols = slice(co, co + C)
            act[g][here, cols] = (a * rd).astype(BF16)
            ub = u.astype(BF16)
            ups[g][here, cols] = ub
            if g:
                there = pl.ds(r + E - ro, 16)
                ups_s[g][there, cols] = ub if m < 0 else -ub

    yield from loop_parts(step, PARTS[l])


def plane(act, ups, ws, msg, back):
    msg[0][...] = dot(act[0][...], ws[0][...])
    back[0][...] = dot_nt(ups[0][...], ws[0][...])
    for g in (1, 2):
        a = act[g][...]
        y0 = dot(a, ws[g][0])
        y1 = dot(a, ws[g][1])
        msg[g][:E, :] = y0[:E] - y1[E:]
        msg[g][E:, :] = y0[E:] + y1[:E]
        u = ups[g][...]
        z0 = dot_nt(u, ws[g][0])
        z1 = dot_nt(u, ws[g][1])
        back[g][:E, :] = z0[:E] + z1[E:]
        back[g][E:, :] = z0[E:] - z1[:E]


def rotate_out(l, msg, back, rad, wide, oh_st, oh_dt, m_buf, e_buf, out, grad):
    size = 2 * l + 1

    def step(b):
        r = pl.multiple_of(b * 16, 16)
        rows = pl.ds(r, 16)
        rd = rad[rows, l * C : (l + 1) * C].astype(F32)
        ms, bs = [], []
        for m in orders(l):
            g, ro, co = group_slot(l, m)
            here = pl.ds(r + ro, 16)
            ms.append(msg[g][here, co : co + C])
            bs.append(back[g][here, co : co + C] * rd)
        n = len(ms)
        for i in range(size):
            a = u = None
            for j in range(n):
                w = wide[kept(l) + j * size + i, rows, :]
                a = w * ms[j] if a is None else a + w * ms[j]
                u = w * bs[j] if u is None else u + w * bs[j]
            m_buf[rows, i * C : (i + 1) * C] = a.astype(BF16)
            e_buf[rows, i * C : (i + 1) * C] = u.astype(BF16)

    yield from loop_parts(step, PARTS[l])
    cols = slice(l * l * C, (l + 1) * (l + 1) * C)
    shape = (4, 4, 16, size * C)
    out[:, :, :, cols] = dot(oh_dt[...], m_buf[:, : size * C]).astype(BF16).reshape(shape)
    grad[:, :, :, cols] = dot(oh_st[...], e_buf[:, : size * C]).astype(BF16).reshape(shape)


def weight_grads(act, ups, ups_s, flat):
    scale = 1.0 / math.sqrt(32768)
    at = 0
    for g in range(3):
        left = act[g][...].T
        for right in (ups, ups_s)[: 1 if g == 0 else 2]:
            total = (dot(left, right[g][...]) * scale).astype(BF16)
            rows = total.shape[0]
            for c in range(rows // C):
                flat[at : at + rows // 16] = total[:, c * C : (c + 1) * C].reshape(rows // 16, 16, C)
                at += rows // 16
    flat[600:608] = jnp.zeros((8, 16, C), BF16)


MESH = pl.DeviceIdType.MESH
TILES = 304
HALVES = ((0, 10), (160, 9))


def start_at(z):
    return lax.div(z * 16, 7) if not isinstance(z, int) else z * 16 // 7


def wrap(p, d, n):
    return lax.rem(p + (d % n), n)


class Place:
    def __init__(self):
        g, p = lax.axis_index("graph"), lax.axis_index("dp")
        self.g, self.p = g, p
        self.y, self.x = lax.div(g, 4), lax.rem(g, 4)
        self.z, self.c = lax.div(p, 2), lax.rem(p, 2)

    def plane(self, dy, dx):
        return (self.p, wrap(self.y, dy, 4) * 4 + wrap(self.x, dx, 4))

    def peer(self, d):
        return (self.p, wrap(self.g, d, 16))

    def up(self, d):
        return (wrap(self.z, d, 8) * 2 + self.c, self.g)

    def sibling(self):
        return (self.z * 2 + 1 - self.c, self.g)


class Sender:
    def __init__(self, send, recv):
        self.send, self.recv, self.next, self.open, self.most = send, recv, 0, [], 0

    def go(self, src, dst, to):
        c = pltpu.make_async_remote_copy(src_ref=src, dst_ref=dst, send_sem=self.send.at[len(self.open)],
                                         recv_sem=self.recv.at[self.next], device_id=to, device_id_type=MESH)
        self.next += 1
        self.open.append(c)
        c.start()
        return c

    def drain(self):
        for c in self.open:
            c.wait_send()
        self.open = []


class Runner:
    def __init__(self):
        self.active = []

    def add(self, stream, delay=0):
        self.active.append([stream, delay])
        return stream

    def run(self):
        while self.active:
            for entry in list(self.active):
                if entry[1] > 0:
                    entry[1] -= 1
                    continue
                try:
                    next(entry[0])
                except StopIteration:
                    self.active.remove(entry)


def gather_stream(snd, at, dev):
    def spread(da):
        return [snd.go(at(da, 0, None), at(da, 0, None), dev(0, s)) for s in (1, -1)]

    def relay(da, got):
        for k, s in enumerate((1, -1)):
            yield
            got[k].wait_recv()
            last.append(snd.go(at(da, -s, k), at(da, -s, k), dev(0, s)))

    last = []
    first = {-s: snd.go(at(0, 0, None), at(0, 0, None), dev(s, 0)) for s in (1, -1)}
    second = {0: spread(0)}
    first[2] = snd.go(at(0, 0, None), at(0, 0, None), dev(2, 0))
    for da in (-1, 1):
        yield
        first[da].wait_recv()
        second[da] = spread(da)
    yield from relay(0, second[0])
    yield
    first[2].wait_recv()
    second[2] = spread(2)
    for da in (-1, 1, 2):
        yield from relay(da, second[da])
    for f in last:
        yield
        f.wait_recv()


def col_at(buf, here, lo, hi, y_first):
    mid = (lo + hi) // 2
    parts = {None: (lo, hi), 0: (lo, mid), 1: (mid, hi)}

    def at(da, db, part):
        dy, dx = (da, db) if y_first else (db, da)
        a, b = parts[part]
        return buf.at[wrap(here.y, dy, 4), wrap(here.x, dx, 4), :, a * C : b * C]
    return at


def plane_dev(here, y_first):
    return (lambda da, db: here.plane(da, db)) if y_first else (lambda da, db: here.plane(db, da))


def add(*xs):
    t = xs[0].astype(F32)
    for x in xs[1:]:
        t = t + x.astype(F32)
    return t.astype(BF16)


def scatter_stream(snd, part, mid, t, r, q, r2, out, here, lo, hi, y_first):
    cm = (lo + hi) // 2
    full, halves = slice(lo * C, hi * C), (slice(lo * C, cm * C), slice(cm * C, hi * C))
    a, b = (here.y, here.x) if y_first else (here.x, here.y)
    dev = plane_dev(here, y_first)

    def row(da, cols):
        i = wrap(a, da, 4)
        return part.at[i, :, :, cols] if y_first else part.at[:, i, :, cols]

    got = [snd.go(row(2, halves[k]), t.at[k, :, :, halves[k]], dev(s, 0)) for k, s in enumerate((1, -1))]
    sent = []
    for k, s in enumerate((1, -1)):
        yield
        got[k].wait_recv()
        mid[k, :, :, halves[k]] = add(row(s, halves[k])[...], t[k, :, :, halves[k]])
        mid[k, :, :, halves[1 - k]] = row(s, halves[1 - k])[...]
        sent.append(snd.go(mid.at[k, :, :, full], r.at[k, :, :, full], dev(s, 0)))
    yield
    sent[0].wait_recv()
    sent[1].wait_recv()
    q[:, :, full] = add(row(0, full)[...], r[0, :, :, full], r[1, :, :, full])
    sent = []
    for k, s in enumerate((2, 1, -1)):
        sent.append(snd.go(q.at[wrap(b, s, 4), :, full], r2.at[k, :, full], dev(0, s)))
    yield
    for c in sent:
        c.wait_recv()
    out[:, full] = add(q[b, :, full], *(r2[k, :, full] for k in range(3)))


def block(ref, base, size, a, b, count=1):
    return ref.at[pl.ds(base + (a * 4 + b) * size, size * count)]


def weight_start(snd, flat, sib, here):
    other = (1 - here.c) * TILES
    copies = {}
    for da in (2, 1, -1, 0):
        for part, (off, size) in enumerate(HALVES):
            a = wrap(here.y if part == 0 else here.x, da, 4)
            copies[part, da] = snd.go(block(flat, other + off, size, a, 0, 4), block(sib, off, size, a, 0, 4), here.sibling())
    return copies


def weight_plane(snd, copies, part, flat, sib, hsum, tbox, qsum, t2box, zin, here):
    off, size = HALVES[part]
    y_first = part == 0
    a, b = (here.y, here.x) if y_first else (here.x, here.y)
    dev = plane_dev(here, y_first)
    own = here.c * TILES
    sent = []
    for k, da in enumerate((2, 1, -1)):
        copies[part, da].wait_recv()
        i = wrap(a, da, 4)
        block(hsum, off, size, i, 0, 4)[...] = add(block(flat, own + off, size, i, 0, 4)[...], block(sib, off, size, i, 0, 4)[...])
        sent.append(snd.go(block(hsum, off, size, i, 0, 4), tbox.at[k, off // 4 : off // 4 + 4 * size], dev(da, 0)))
    copies[part, 0].wait_recv()
    yield
    for c in sent:
        c.wait_recv()
    rows = slice(off // 4, off // 4 + 4 * size)
    qsum[rows] = add(block(flat, own + off, size, a, 0, 4)[...], block(sib, off, size, a, 0, 4)[...], *(tbox[k, rows] for k in range(3)))
    sent = []
    for k, db in enumerate((2, 1, -1)):
        i = wrap(b, db, 4)
        sent.append(snd.go(qsum.at[pl.ds(off // 4 + i * size, size)], t2box.at[k, off // 16 : off // 16 + size], dev(0, db)))
    yield
    for c in sent:
        c.wait_recv()
    rows = slice(off // 16, off // 16 + size)
    zin[rows] = add(qsum[pl.ds(off // 4 + b * size, size)], *(t2box[k, rows] for k in range(3)))


def weight_z(snd, zin, zbox, zall, zout, res, here):
    copies = [snd.go(zin.at[pl.ds(start_at(wrap(here.z, d, 8)), 3)], zbox.at[d], here.up(d)) for d in range(1, 8)]
    yield
    total = zin[pl.ds(start_at(here.z), 3)].astype(F32)
    for d in range(1, 8):
        copies[d - 1].wait_recv()
        total = total + zbox[d].astype(F32)
    zall[here.z] = total.astype(BF16)
    copies = [snd.go(zall.at[here.z], zall.at[here.z], here.up(d)) for d in range(1, 8)]
    yield
    for c in copies:
        c.wait_recv()
    for z in range(8):
        zout[start_at(z) : start_at(z) + 3] = zall[z]
    for part, (off, size) in enumerate(HALVES):
        a, b = (here.y, here.x) if part == 0 else (here.x, here.y)
        block(res, here.c * TILES + off, size, a, b)[...] = zout[off // 16 : off // 16 + size]


def weight_spread(snd, part, res, here, cores):
    off, size = HALVES[part]
    y_first = part == 0
    a, b = (here.y, here.x) if y_first else (here.x, here.y)
    dev = plane_dev(here, y_first)

    def at(da, db):
        return block(res, here.c * TILES + off, size, wrap(a, da, 4), wrap(b, db, 4))

    def to_core(da):
        row = block(res, here.c * TILES + off, size, wrap(a, da, 4), 0, 4)
        cores.append(snd.go(row, row, here.sibling()))

    first = {-d % 4: snd.go(at(0, 0), at(0, 0), dev(d, 0)) for d in (1, -1, 2)}
    second = {}
    for db in (1, -1, 2):
        second[0, -db % 4] = snd.go(at(0, 0), at(0, 0), dev(0, db))
    for da in (1, 3, 2):
        yield
        first[da].wait_recv()
        for db in (1, -1, 2):
            second[da, -db % 4] = snd.go(at(da, 0), at(da, 0), dev(0, db))
    for da in (0, 1, 3, 2):
        yield
        for db in (1, 3, 2):
            second[da, db].wait_recv()
        to_core(da)


CHUNKS = (((0, 1, 2), 0), ((3,), 2), ((4,), 4))
RCHUNKS = ((4,), (3,), (0, 1, 2))
ORDER = "wnnwnwn"


def bounds(degrees):
    return degrees[0] ** 2, (degrees[-1] + 1) ** 2


def block_kernel(count, src_in, dst_in, rot_in, rad_in, f_in, c_in, w0_in, w1_in, w2_in, out, grad, res,
                 src, dst, rot, rad, f_buf, c_buf, oh_s, oh_d, oh_st, oh_dt, rot_t, x_buf, u_buf, wide, a0, a1, a2, u0, u1, u2, v1, v2,
                 m0, m1, m2, b0, b1, b2, mb, eb, w0, w1, w2, p_out, p_grad, mid, t, r, q, r2,
                 flat, sib, hsum, tbox, qsum, t2box, zin, zbox, zall, zout, send, recv, w_sem):
    here = Place()
    loads = [pltpu.make_async_copy(i, o, w_sem.at[k]) for k, (i, o) in enumerate((
        (f_in.at[0], f_buf.at[here.y, here.x]), (c_in.at[0], c_buf.at[here.y, here.x]), (src_in, src), (dst_in, dst),
        (rot_in, rot), (rad_in, rad), (w0_in, w0), (w1_in, w1), (w2_in, w2)))]
    for c in loads:
        c.start()
    partners = [here.sibling()] + [here.up(d) for d in range(1, 8)] + [here.peer(d) for d in range(1, 16)]
    barrier = pltpu.get_barrier_semaphore()
    for d in partners:
        pl.semaphore_signal(barrier, inc=1, device_id=d, device_id_type=MESH)
    for c in loads[:5]:
        c.wait()
    prepare(src[...], dst[...], count[0, 0], rot[...], oh_s, oh_d, oh_st, oh_dt, rot_t)
    pl.semaphore_wait(barrier, len(partners))
    loads[5].wait()

    act, ups, ups_s = (a0, a1, a2), (u0, u1, u2), (None, v1, v2)
    ws, msg, back = (w0, w1, w2), (m0, m1, m2), (b0, b1, b2)
    snd = Sender(send, recv)
    run = Runner()

    def take_in(degrees, parts):
        for p in parts:
            yield from p
        for l in degrees:
            yield
            yield from rotate_in(l, f_buf, c_buf, oh_s, oh_d, rad, rot_t, x_buf, u_buf, wide, act, ups, ups_s)

    def both(lo, hi):
        f = gather_stream(snd, col_at(f_buf, here, lo, hi, False), plane_dev(here, False))
        c = gather_stream(snd, col_at(c_buf, here, lo, hi, True), plane_dev(here, True))
        live = [f, c]
        while live:
            for s in list(live):
                try:
                    next(s)
                except StopIteration:
                    live.remove(s)
            if live:
                yield

    starts = []
    for degrees, delay in CHUNKS:
        stream = both(*bounds(degrees))
        next(stream)
        run.add(take_in(degrees, [stream]), delay)
    run.run()

    weight_grads(act, ups, ups_s, flat)
    snd.drain()
    copies = weight_start(snd, flat, sib, here)

    def turns(streams):
        live = list(streams)
        while live:
            for s in list(live):
                try:
                    next(s)
                except StopIteration:
                    live.remove(s)
            yield

    def weights():
        yield from turns([weight_plane(snd, copies, p, flat, sib, hsum, tbox, qsum, t2box, zin, here) for p in range(2)])
        yield from weight_z(snd, zin, zbox, zall, zout, res, here)
        cores = []
        yield from turns([weight_spread(snd, p, res, here, cores) for p in range(2)])
        for c in cores:
            c.wait_recv()

    sums = weights()
    rows = []
    for c in loads[6:]:
        c.wait()
    plane(act, ups, ws, msg, back)
    for k, degrees in enumerate(RCHUNKS):
        for l in degrees:
            for _ in rotate_out(l, msg, back, rad, wide, oh_st, oh_dt, mb, eb, p_out, p_grad):
                pass
        lo, hi = bounds(degrees)
        for i, (part, dst_ref, yf) in enumerate(((p_out, out, True), (p_grad, grad, False))):
            rows.append(scatter_stream(snd, part, mid.at[i], t.at[i], r.at[i], q.at[i], r2.at[i], dst_ref, here, lo, hi, yf))
            next(rows[-1])
        if k == 0:
            next(sums)
    for step in ORDER:
        if step == "w":
            next(sums, None)
        else:
            for s in rows:
                next(s, None)
    for _ in sums:
        pass
    snd.drain()


def edge_block(count, src, dst, rot, rad, feats, cots, w0, w1, w2):
    v = pl.BlockSpec(memory_space=pltpu.VMEM)
    h = pl.BlockSpec(memory_space=pltpu.HBM)
    V = pltpu.VMEM
    rows = jax.ShapeDtypeStruct((16, W), BF16)
    n_send, n_recv = 114, 228
    return pl.pallas_call(
        block_kernel,
        out_shape=(rows, rows, jax.ShapeDtypeStruct((2 * TILES, 16, C), BF16)),
        in_specs=[pl.BlockSpec(memory_space=pltpu.SMEM)] + [h] * 9,
        out_specs=(v,) * 3,
        scratch_shapes=[
            V((1, E), jnp.int32), V((1, E), jnp.int32), V((165, E), BF16), V((E, 640), BF16),
            V((4, 4, 16, W), BF16), V((4, 4, 16, W), BF16),
            V((E, N), BF16), V((E, N), BF16), V((N, E), BF16), V((N, E), BF16), V((E, 256), F32),
            V((E, 9 * C), F32), V((E, 9 * C), F32), V((115, E, C), F32),
            V((E, 640), BF16), V((2 * E, 512), BF16), V((2 * E, 384), BF16),
            V((E, 640), BF16), V((2 * E, 512), BF16), V((2 * E, 384), BF16),
            V((2 * E, 512), BF16), V((2 * E, 384), BF16),
            V((E, 640), F32), V((2 * E, 512), F32), V((2 * E, 384), F32),
            V((E, 640), F32), V((2 * E, 512), F32), V((2 * E, 384), F32),
            V((E, 9 * C), BF16), V((E, 9 * C), BF16),
            V((640, 640), BF16), V((2, 512, 512), BF16), V((2, 384, 384), BF16),
            V((4, 4, 16, W), BF16), V((4, 4, 16, W), BF16),
            V((2, 2, 4, 16, W), BF16), V((2, 2, 4, 16, W), BF16), V((2, 2, 4, 16, W), BF16), V((2, 4, 16, W), BF16),
            V((2, 3, 16, W), BF16),
            V((2 * TILES, 16, C), BF16), V((TILES, 16, C), BF16), V((TILES, 16, C), BF16), V((3, 76, 16, C), BF16),
            V((76, 16, C), BF16), V((3, 19, 16, C), BF16), V((19, 16, C), BF16), V((8, 3, 16, C), BF16), V((8, 3, 16, C), BF16),
            V((19, 16, C), BF16),
            pltpu.SemaphoreType.DMA((n_send,)), pltpu.SemaphoreType.DMA((n_recv,)), pltpu.SemaphoreType.DMA((9,)),
        ],
        compiler_params=pltpu.CompilerParams(collective_id=0, has_side_effects=True, vmem_limit_bytes=60 * 2**20),
        name="edge_block",
    )(count, src, dst, rot, rad, feats, cots, w0, w1, w2)


def finish_kernel(rows_in, grad_in, flat, rows, grad, g0, g1, g2):
    rows[0] = rows_in[...]
    grad[0] = grad_in[...]
    for c in range(5):
        g0[:, c * C : (c + 1) * C] = flat[c * 40 : c * 40 + 40].reshape(640, C).astype(F32)
    for i in range(2):
        for c in range(4):
            b = 200 + i * 128 + c * 32
            g1[i, :, c * C : (c + 1) * C] = flat[b : b + 32].reshape(512, C).astype(F32)
        for c in range(3):
            b = 456 + i * 72 + c * 24
            g2[i, :, c * C : (c + 1) * C] = flat[b : b + 24].reshape(384, C).astype(F32)


def finish(rows, grad, flat):
    v = pl.BlockSpec(memory_space=pltpu.VMEM)
    o = jax.ShapeDtypeStruct((1, 16, W), BF16)
    return pl.pallas_call(
        finish_kernel,
        out_shape=(o, o, jax.ShapeDtypeStruct((640, 640), F32), jax.ShapeDtypeStruct((2, 512, 512), F32),
                   jax.ShapeDtypeStruct((2, 384, 384), F32)),
        in_specs=[v] * 3, out_specs=(v,) * 5,
        compiler_params=pltpu.CompilerParams(vmem_limit_bytes=60 * 2**20),
        name="finish",
    )(rows, grad, flat)


def per_device(node_feats, source, target, rotation, radial, edge_count, cotangent, weight_zero, weight_first, weight_second):
    rows, grad, flat = edge_block(
        edge_count, source, target, rotation[0], radial[0], node_feats, cotangent, weight_zero, weight_first, weight_second)
    return tuple(finish(rows, grad, flat))


def solution(mesh):
    edge = P("dp", "graph")
    node = P("dp", "graph", None)
    return jax.shard_map(
        per_device,
        mesh=mesh,
        in_specs=(node, edge, edge, P("dp", None, "graph"), node, edge, node, P(), P(), P()),
        out_specs=(node, node, P(), P(), P()),
        check_vma=False,
    )
```

time: 135 us -> 100 us (0.74)
  Pallas kernels: 120 us -> 98.9 us
  local copies, waits for them, and re-layouts: 13.1 us -> 0 us
    pallas_call x3 -> x2, Pallas kernels: 120 us -> 98.9 us  [the longest x1 94.5 us: edge_block(): pl.pallas_call(block_kernel, out_shape=(rows, rows, jax.ShapeDtypeStruct(...]
    unnamed x17 -> x0, local copies, waits for them, and re-layouts: 13.1 us -> none
where the time goes in v2:
time: 100 us
  Pallas kernels  98.9 us (99%)
  between operations  1.29 us (1%)
    pallas_call x1, Pallas kernels, edge_block(): pl.pallas_call(block_kernel, out_shape=(rows, rows, jax.ShapeDtypeStruct(...  94.5 us
    pallas_call x1, Pallas kernels, finish(): pl.pallas_call(finish_kernel, out_shape=(o, o, jax.ShapeDtypeStruct((640,...  4.39 us

profile of v2, /device:TPU:1, one launch (start us, length us, event | category | flops | bytes accessed | tf_op | source)
XLA Modules:
  0.0 100.2 jit_solution(13522860453933123432)
XLA Ops:
  1.3 94.5 %edge_block.1 = (bf16[16,3200]{1,0:T(8,128)(2,1)}, bf16[16,3200]{1,0:T(8,128)(2,1)}, bf16[608,16,128]{2,1,0:T(8,128)(2,1)}) custom-call(s32[1,1]{1,0:T(1,128)S(6)} %copy.15.count, s32[1,128]{1,0:T(1,128)} %src_in.1, s32[1,128]{1,0:T(1,128)} %dst_in.1, bf16[165,128]{1,0:T(8,128)(2,1)} %bitcast.3, bf16[128,640]{1,0:T(8,128)(2,1)} %bitcast.2, ...), custom_call_target="tpu_custom_call" | custom-call | tf_op jit(solution)/shard_map/edge_block/pallas_call | solution.py:523
  95.8 4.4 %finish.1 = (bf16[1,16,3200]{2,1,0:T(8,128)(2,1)}, bf16[1,16,3200]{2,1,0:T(8,128)(2,1)}, f32[640,640]{1,0:T(8,128)}, f32[2,512,512]{2,1,0:T(8,128)}, f32[2,384,384]{2,1,0:T(8,128)}) custom-call(bf16[16,3200]{1,0:T(8,128)(2,1)} %get-tuple-element.8.rows_in, bf16[16,3200]{1,0:T(8,128)(2,1)} %get-tuple-element.9.grad_in, ...), custom_call_target="tpu_custom_call" | custom-call | tf_op jit(solution)/shard_map/finish/pallas_call | solution.py:570

commit v3 on v2

--- a/solution.py
+++ b/solution.py
@@ -408,6 +408,7 @@
 CHUNKS = (((0, 1, 2), 0), ((3,), 2), ((4,), 4))
 RCHUNKS = ((4,), (3,), (0, 1, 2))
 ORDER = "wnnwnwn"
+FIRST = 1
 
 
 def bounds(degrees):
@@ -424,7 +425,8 @@
         (rot_in, rot), (rad_in, rad), (w0_in, w0), (w1_in, w1), (w2_in, w2)))]
     for c in loads:
         c.start()
-    partners = [here.sibling()] + [here.up(d) for d in range(1, 8)] + [here.peer(d) for d in range(1, 16)]
+    partners = [here.sibling()] + [here.up(d) for d in range(1, 8)] + [
+        here.plane(*d) for d in ((0, 1), (0, -1), (0, 2), (1, 0), (-1, 0), (2, 0))]
     barrier = pltpu.get_barrier_semaphore()
     for d in partners:
         pl.semaphore_signal(barrier, inc=1, device_id=d, device_id_type=MESH)
@@ -494,6 +496,8 @@
         c.wait()
     plane(act, ups, ws, msg, back)
     for k, degrees in enumerate(RCHUNKS):
+        if k == FIRST:
+            next(sums)
         for l in degrees:
             for _ in rotate_out(l, msg, back, rad, wide, oh_st, oh_dt, mb, eb, p_out, p_grad):
                 pass
@@ -501,8 +505,6 @@
         for i, (part, dst_ref, yf) in enumerate(((p_out, out, True), (p_grad, grad, False))):
             rows.append(scatter_stream(snd, part, mid.at[i], t.at[i], r.at[i], q.at[i], r2.at[i], dst_ref, here, lo, hi, yf))
             next(rows[-1])
-        if k == 0:
-            next(sums)
     for step in ORDER:
         if step == "w":
             next(sums, None)
@@ -550,28 +552,47 @@
     )(count, src, dst, rot, rad, feats, cots, w0, w1, w2)
 
 
-def finish_kernel(rows_in, grad_in, flat, rows, grad, g0, g1, g2):
+def finish_kernel(rows_in, grad_in, flat_in, rows, grad, g0_out, g1_out, g2_out, flat, g0, g1, g2, sems):
+    parts = ((0, 200), (200, 256), (456, 144))
+    ends = []
+    loads = [pltpu.make_async_copy(flat_in.at[b : b + n], flat.at[b : b + n], sems.at[k]) for k, (b, n) in enumerate(parts)]
+    for c in loads:
+        c.start()
     rows[0] = rows_in[...]
     grad[0] = grad_in[...]
+
+    def send(k, src, dst):
+        c = pltpu.make_async_copy(src, dst, sems.at[3 + k])
+        c.start()
+        ends.append(c)
+
+    loads[0].wait()
     for c in range(5):
         g0[:, c * C : (c + 1) * C] = flat[c * 40 : c * 40 + 40].reshape(640, C).astype(F32)
-    for i in range(2):
-        for c in range(4):
-            b = 200 + i * 128 + c * 32
-            g1[i, :, c * C : (c + 1) * C] = flat[b : b + 32].reshape(512, C).astype(F32)
-        for c in range(3):
-            b = 456 + i * 72 + c * 24
-            g2[i, :, c * C : (c + 1) * C] = flat[b : b + 24].reshape(384, C).astype(F32)
+    send(0, g0, g0_out)
+    for k, (width, g, g_out) in enumerate(((4, g1, g1_out), (3, g2, g2_out))):
+        loads[k + 1].wait()
+        at = parts[k + 1][0]
+        for i in range(2):
+            for c in range(width):
+                g[i, :, c * C : (c + 1) * C] = flat[at : at + 8 * width].reshape(width * C, C).astype(F32)
+                at += 8 * width
+            send(1 + 2 * k + i, g.at[i], g_out.at[i])
+    for c in ends:
+        c.wait()
 
 
 def finish(rows, grad, flat):
+    h = pl.BlockSpec(memory_space=pltpu.HBM)
     v = pl.BlockSpec(memory_space=pltpu.VMEM)
+    V = pltpu.VMEM
     o = jax.ShapeDtypeStruct((1, 16, W), BF16)
+    shapes = ((640, 640), (2, 512, 512), (2, 384, 384))
     return pl.pallas_call(
         finish_kernel,
-        out_shape=(o, o, jax.ShapeDtypeStruct((640, 640), F32), jax.ShapeDtypeStruct((2, 512, 512), F32),
-                   jax.ShapeDtypeStruct((2, 384, 384), F32)),
-        in_specs=[v] * 3, out_specs=(v,) * 5,
+        out_shape=(o, o) + tuple(jax.ShapeDtypeStruct(s, F32) for s in shapes),
+        in_specs=[v, v, h], out_specs=(v, v, h, h, h),
+        scratch_shapes=[V((2 * TILES, 16, C), BF16)] + [V(s, F32) for s in shapes] + [pltpu.SemaphoreType.DMA((8,))],
         compiler_params=pltpu.CompilerParams(vmem_limit_bytes=60 * 2**20),
         name="finish",
     )(rows, grad, flat)

time: 100 us -> 100 us (level)
  no operation moved by 1% of the time
where the time goes in v3:
time: 100 us
  Pallas kernels  98.7 us (99%)
  between operations  1.29 us (1%)
    pallas_call x1, Pallas kernels, edge_block(): pl.pallas_call(block_kernel, out_shape=(rows, rows, jax.ShapeDtypeStruct(...  93.5 us
    pallas_call x1, Pallas kernels, finish(): pl.pallas_call(finish_kernel, out_shape=(o, o) + tuple((jax.ShapeDtypeStr...  5.18 us

profile of v3, /device:TPU:1, one launch (start us, length us, event | category | flops | bytes accessed | tf_op | source)
XLA Modules:
  0.0 100.0 jit_solution(3358975913921478336)
XLA Ops:
  1.3 93.5 %edge_block.1 = (bf16[16,3200]{1,0:T(8,128)(2,1)}, bf16[16,3200]{1,0:T(8,128)(2,1)}, bf16[608,16,128]{2,1,0:T(8,128)(2,1)}) custom-call(s32[1,1]{1,0:T(1,128)S(6)} %copy.15.count, s32[1,128]{1,0:T(1,128)} %src_in.1, s32[1,128]{1,0:T(1,128)} %dst_in.1, bf16[165,128]{1,0:T(8,128)(2,1)} %bitcast.3, bf16[128,640]{1,0:T(8,128)(2,1)} %bitcast.2, ...), custom_call_target="tpu_custom_call" | custom-call | tf_op jit(solution)/shard_map/edge_block/pallas_call | solution.py:525
  94.8 5.2 %finish.1 = (bf16[1,16,3200]{2,1,0:T(8,128)(2,1)}, bf16[1,16,3200]{2,1,0:T(8,128)(2,1)}, f32[640,640]{1,0:T(8,128)}, f32[2,512,512]{2,1,0:T(8,128)}, f32[2,384,384]{2,1,0:T(8,128)}) custom-call(bf16[16,3200]{1,0:T(8,128)(2,1)} %get-tuple-element.8.rows_in, bf16[16,3200]{1,0:T(8,128)(2,1)} %get-tuple-element.9.grad_in, ...), custom_call_target="tpu_custom_call" | custom-call | tf_op jit(solution)/shard_map/finish/pallas_call | solution.py:591

commit v4 on v2

--- a/solution.py
+++ b/solution.py
@@ -408,6 +408,7 @@
 CHUNKS = (((0, 1, 2), 0), ((3,), 2), ((4,), 4))
 RCHUNKS = ((4,), (3,), (0, 1, 2))
 ORDER = "wnnwnwn"
+FIRST = 1
 
 
 def bounds(degrees):
@@ -424,7 +425,8 @@
         (rot_in, rot), (rad_in, rad), (w0_in, w0), (w1_in, w1), (w2_in, w2)))]
     for c in loads:
         c.start()
-    partners = [here.sibling()] + [here.up(d) for d in range(1, 8)] + [here.peer(d) for d in range(1, 16)]
+    partners = [here.sibling()] + [here.up(d) for d in range(1, 8)] + [
+        here.plane(*d) for d in ((0, 1), (0, -1), (0, 2), (1, 0), (-1, 0), (2, 0))]
     barrier = pltpu.get_barrier_semaphore()
     for d in partners:
         pl.semaphore_signal(barrier, inc=1, device_id=d, device_id_type=MESH)
@@ -494,6 +496,8 @@
         c.wait()
     plane(act, ups, ws, msg, back)
     for k, degrees in enumerate(RCHUNKS):
+        if k == FIRST:
+            next(sums)
         for l in degrees:
             for _ in rotate_out(l, msg, back, rad, wide, oh_st, oh_dt, mb, eb, p_out, p_grad):
                 pass
@@ -501,8 +505,6 @@
         for i, (part, dst_ref, yf) in enumerate(((p_out, out, True), (p_grad, grad, False))):
             rows.append(scatter_stream(snd, part, mid.at[i], t.at[i], r.at[i], q.at[i], r2.at[i], dst_ref, here, lo, hi, yf))
             next(rows[-1])
-        if k == 0:
-            next(sums)
     for step in ORDER:
         if step == "w":
             next(sums, None)

time: 100 us -> 99.4 us (level)
  Pallas kernels: 98.9 us -> 97.9 us
where the time goes in v4:
time: 99.4 us; the launch traced here: 99.2 us
  Pallas kernels  97.9 us (98%)
  between operations  1.29 us (1%)
    pallas_call x1, Pallas kernels, edge_block(): pl.pallas_call(block_kernel, out_shape=(rows, rows, jax.ShapeDtypeStruct(...  93.5 us
    pallas_call x1, Pallas kernels, finish(): pl.pallas_call(finish_kernel, out_shape=(o, o, jax.ShapeDtypeStruct((640,...  4.39 us

profile of v4, /device:TPU:1, one launch (start us, length us, event | category | flops | bytes accessed | tf_op | source)
XLA Modules:
  0.0 99.2 jit_solution(5985667124951896688)
XLA Ops:
  1.3 93.5 %edge_block.1 = (bf16[16,3200]{1,0:T(8,128)(2,1)}, bf16[16,3200]{1,0:T(8,128)(2,1)}, bf16[608,16,128]{2,1,0:T(8,128)(2,1)}) custom-call(s32[1,1]{1,0:T(1,128)S(6)} %copy.15.count, s32[1,128]{1,0:T(1,128)} %src_in.1, s32[1,128]{1,0:T(1,128)} %dst_in.1, bf16[165,128]{1,0:T(8,128)(2,1)} %bitcast.3, bf16[128,640]{1,0:T(8,128)(2,1)} %bitcast.2, ...), custom_call_target="tpu_custom_call" | custom-call | tf_op jit(solution)/shard_map/edge_block/pallas_call | solution.py:525
  94.8 4.4 %finish.1 = (bf16[1,16,3200]{2,1,0:T(8,128)(2,1)}, bf16[1,16,3200]{2,1,0:T(8,128)(2,1)}, f32[640,640]{1,0:T(8,128)}, f32[2,512,512]{2,1,0:T(8,128)}, f32[2,384,384]{2,1,0:T(8,128)}) custom-call(bf16[16,3200]{1,0:T(8,128)(2,1)} %get-tuple-element.8.rows_in, bf16[16,3200]{1,0:T(8,128)(2,1)} %get-tuple-element.9.grad_in, ...), custom_call_target="tpu_custom_call" | custom-call | tf_op jit(solution)/shard_map/finish/pallas_call | solution.py:572
